TPU v7x, 32 devices: a whole 2x2x4 slice. The times are simulated.
32 devices in a mesh: replica: 16 (over z, y, x), group: 2 (over core).
Axes of the slice: x: 2, y: 2, z: 4, core: 2. Of those that a mesh axis runs over, the one named last changes fastest.
Arguments:
- tokens: bfloat16 [24576, 896], P(('replica', 'group')), may hold values from -6 to 6
- cotangent: bfloat16 [24576, 896], P(('replica', 'group')), may hold values from -6 to 6
- first_gain: bfloat16 [896], P('group'), may hold values from 0.5 to 1.5
- query_weight: bfloat16 [896, 896], P('group'), may hold values from -0.1875 to 0.1875
- query_bias: bfloat16 [896], P('group'), may hold values from -2 to 2
- key_weight: bfloat16 [896, 128], P('group'), may hold values from -0.1875 to 0.1875
- key_bias: bfloat16 [128], P('group'), may hold values from -2 to 2
- value_weight: bfloat16 [896, 128], P('group'), may hold values from -0.1875 to 0.1875
- value_bias: bfloat16 [128], P('group'), may hold values from -2 to 2
- output_weight: bfloat16 [896, 896], P('group'), may hold values from -4 to 4
- second_gain: bfloat16 [896], P('group'), may hold values from 0.5 to 1.5
- gate_weight: bfloat16 [896, 4864], P('group'), may hold values from -0.1875 to 0.1875
- up_weight: bfloat16 [896, 4864], P('group'), may hold values from -0.1875 to 0.1875
- down_weight: bfloat16 [4864, 896], P('group'), may hold values from -0.078125 to 0.078125
Outputs:
- block_output: bfloat16 [24576, 896], P(('replica', 'group'))
- input_grad: float32 [24576, 896], P(('replica', 'group'))
- first_gain_grad: float32 [896], P('group')
- query_weight_grad: float32 [896, 896], P('group')
- query_bias_grad: float32 [896], P('group')
- key_weight_grad: float32 [896, 128], P('group')
- key_bias_grad: float32 [128], P('group')
- value_weight_grad: float32 [896, 128], P('group')
- value_bias_grad: float32 [128], P('group')
- output_weight_grad: float32 [896, 896], P('group')
- second_gain_grad: float32 [896], P('group')
- gate_weight_grad: float32 [896, 4864], P('group')
- up_weight_grad: float32 [896, 4864], P('group')
- down_weight_grad: float32 [4864, 896], P('group')
All inputs are finite; a program needn't handle non-finite values.
Results may differ from a plain program's by a relative error of at most 0.019.
Values may be sent and summed in bfloat16 or wider, within the bound.
A program may use at most 384 MiB of HBM per device.

v0:
```python
import math

import jax
import jax.numpy as jnp
from jax import lax
from jax.sharding import PartitionSpec as P

H = 14
KVH = 2
HD = 64


norm_eps = 1e-06
rope_base = 1000000.0
masked_score = -1e30


def tables(positions, width):
    half = width // 2
    freqs = rope_base ** (-(jnp.arange(half, dtype=jnp.float32) * 2.0 / width))
    angles = positions.astype(jnp.float32)[:, None] * freqs[None, :]
    cosine = jnp.concatenate([jnp.cos(angles), jnp.cos(angles)], axis=-1)[:, None, :]
    sine = jnp.concatenate([jnp.sin(angles), jnp.sin(angles)], axis=-1)[:, None, :]
    return (cosine, sine)


def rotate(field, cosine, sine):
    half = field.shape[-1] // 2
    turned = jnp.concatenate([-field[..., half:], field[..., :half]], axis=-1)
    return field * cosine + turned * sine


def unrotate(grad, cosine, sine):
    half = grad.shape[-1] // 2
    moved = grad * sine
    return grad * cosine + jnp.concatenate([moved[..., half:], -moved[..., :half]], axis=-1)


def norm_back(grad_hidden, normed, inverse, gain):
    scaled = grad_hidden * gain.astype(jnp.float32)
    gain_grad = jnp.sum(grad_hidden * normed, axis=0)
    return (
        gain_grad,
        inverse * (scaled - normed * jnp.mean(scaled * normed, axis=-1, keepdims=True)),
    )


def local(
    tokens,
    cotangent,
    first_gain,
    query_weight,
    query_bias,
    key_weight,
    key_bias,
    value_weight,
    value_bias,
    output_weight,
    second_gain,
    gate_weight,
    up_weight,
    down_weight,
):
    gathered = (
        lax.all_gather(first_gain, "group", axis=0, tiled=True),
        lax.all_gather(query_weight, "group", axis=0, tiled=True),
        lax.all_gather(query_bias, "group", axis=0, tiled=True),
        lax.all_gather(key_weight, "group", axis=0, tiled=True),
        lax.all_gather(key_bias, "group", axis=0, tiled=True),
        lax.all_gather(value_weight, "group", axis=0, tiled=True),
        lax.all_gather(value_bias, "group", axis=0, tiled=True),
        lax.all_gather(output_weight, "group", axis=0, tiled=True),
        lax.all_gather(second_gain, "group", axis=0, tiled=True),
        lax.all_gather(gate_weight, "group", axis=0, tiled=True),
        lax.all_gather(up_weight, "group", axis=0, tiled=True),
        lax.all_gather(down_weight, "group", axis=0, tiled=True),
    )
    (
        gain_one,
        query_mat,
        query_add,
        key_mat,
        key_add,
        value_mat,
        value_add,
        out_mat,
        gain_two,
        gate_mat,
        up_mat,
        down_mat,
    ) = gathered
    rows = tokens.shape[0]
    spread = lax.axis_size("group")
    rank = lax.axis_index("group")
    ratio = H // KVH
    scale = 1.0 / math.sqrt(HD)
    residual = tokens.astype(jnp.float32)
    inv_one = lax.rsqrt(jnp.mean(residual * residual, axis=-1, keepdims=True) + norm_eps)
    normed_one = residual * inv_one
    hidden_one = (normed_one * gain_one.astype(jnp.float32)).astype(jnp.bfloat16)
    queries = jnp.dot(hidden_one, query_mat, preferred_element_type=jnp.float32) + query_add.astype(
        jnp.float32
    )
    keys_pre = jnp.dot(hidden_one, key_mat, preferred_element_type=jnp.float32) + key_add.astype(
        jnp.float32
    )
    values_pre = jnp.dot(
        hidden_one, value_mat, preferred_element_type=jnp.float32
    ) + value_add.astype(jnp.float32)
    query_pos = rank * rows + jnp.arange(rows, dtype=jnp.int32)
    key_pos = jnp.arange(rows * spread, dtype=jnp.int32)
    cosine, sine = tables(query_pos, HD)
    query_rot = rotate(queries.reshape(rows, H, HD), cosine, sine).astype(jnp.bfloat16)
    key_rot = rotate(keys_pre.reshape(rows, KVH, HD), cosine, sine).astype(jnp.bfloat16)
    value_low = values_pre.astype(jnp.bfloat16)
    key_all, value_all = (
        lax.all_gather(key_rot.reshape(rows, KVH * HD), "group", axis=0, tiled=True),
        lax.all_gather(value_low, "group", axis=0, tiled=True),
    )
    key_all = key_all.reshape(-1, KVH, HD)
    value_all = value_all.reshape(-1, KVH, HD)
    grouped = query_rot.reshape(rows, KVH, ratio, HD)
    allowed = key_pos[None, :] <= query_pos[:, None]

    def scores_of(head):
        raw = (
            jnp.einsum(
                "tgd,sd->gts",
                grouped[:, head],
                key_all[:, head],
                preferred_element_type=jnp.float32,
            )
            * scale
        )
        return jnp.where(allowed[None], raw, masked_score)

    log_totals = []
    attended_heads = []
    for head in range(KVH):
        scores = scores_of(head)
        top = jnp.max(scores, axis=-1, keepdims=True)
        log_total = top + jnp.log(jnp.sum(jnp.exp(scores - top), axis=-1, keepdims=True))
        probs = jnp.exp(scores - log_total)
        attended_heads.append(
            jnp.einsum(
                "gts,sd->tgd",
                probs.astype(jnp.bfloat16),
                value_all[:, head],
                preferred_element_type=jnp.float32,
            )
        )
        log_totals.append(log_total)
    attended = jnp.stack(attended_heads, axis=1)
    attended_low = attended.reshape(rows, H * HD).astype(jnp.bfloat16)
    middle = residual + jnp.dot(attended_low, out_mat, preferred_element_type=jnp.float32)
    inv_two = lax.rsqrt(jnp.mean(middle * middle, axis=-1, keepdims=True) + norm_eps)
    normed_two = middle * inv_two
    hidden_two = (normed_two * gain_two.astype(jnp.float32)).astype(jnp.bfloat16)
    gate_pre = jnp.dot(hidden_two, gate_mat, preferred_element_type=jnp.float32)
    up_pre = jnp.dot(hidden_two, up_mat, preferred_element_type=jnp.float32)
    sigmoid_gate = jax.nn.sigmoid(gate_pre)
    swish = gate_pre * sigmoid_gate
    product = (swish * up_pre).astype(jnp.bfloat16)
    final = middle + jnp.dot(product, down_mat, preferred_element_type=jnp.float32)
    block_output = final.astype(jnp.bfloat16)
    again = (
        lax.all_gather(first_gain, "group", axis=0, tiled=True),
        lax.all_gather(query_weight, "group", axis=0, tiled=True),
        lax.all_gather(key_weight, "group", axis=0, tiled=True),
        lax.all_gather(value_weight, "group", axis=0, tiled=True),
        lax.all_gather(output_weight, "group", axis=0, tiled=True),
        lax.all_gather(second_gain, "group", axis=0, tiled=True),
        lax.all_gather(gate_weight, "group", axis=0, tiled=True),
        lax.all_gather(up_weight, "group", axis=0, tiled=True),
        lax.all_gather(down_weight, "group", axis=0, tiled=True),
    )
    gain_one, query_mat, key_mat, value_mat, out_mat, gain_two, gate_mat, up_mat, down_mat = again
    upstream_f = cotangent.astype(jnp.float32)
    down_grad = jnp.einsum("tf,td->fd", product, cotangent, preferred_element_type=jnp.float32)
    product_grad = jnp.einsum("td,fd->tf", cotangent, down_mat, preferred_element_type=jnp.float32)
    gate_grad = (
        product_grad * up_pre * sigmoid_gate * (1.0 + gate_pre * (1.0 - sigmoid_gate))
    ).astype(jnp.bfloat16)
    up_grad = (product_grad * swish).astype(jnp.bfloat16)
    gate_wgrad = jnp.einsum("tc,tf->cf", hidden_two, gate_grad, preferred_element_type=jnp.float32)
    up_wgrad = jnp.einsum("tc,tf->cf", hidden_two, up_grad, preferred_element_type=jnp.float32)
    hidden_two_grad = jnp.einsum(
        "tf,cf->tc", gate_grad, gate_mat, preferred_element_type=jnp.float32
    )
    hidden_two_grad = hidden_two_grad + jnp.einsum(
        "tf,cf->tc", up_grad, up_mat, preferred_element_type=jnp.float32
    )
    gain_two_grad, through_two = norm_back(hidden_two_grad, normed_two, inv_two, gain_two)
    middle_grad = upstream_f + through_two
    branch_grad = middle_grad.astype(jnp.bfloat16)
    out_wgrad = jnp.einsum(
        "tq,td->qd", attended_low, branch_grad, preferred_element_type=jnp.float32
    )
    attended_grad = jnp.einsum(
        "td,qd->tq", branch_grad, out_mat, preferred_element_type=jnp.float32
    ).astype(jnp.bfloat16)
    attended_grad = attended_grad.reshape(rows, KVH, ratio, HD)
    query_heads = []
    key_heads = []
    value_heads = []
    for head in range(KVH):
        scores = scores_of(head)
        probs = jnp.exp(scores - log_totals[head])
        head_grad = attended_grad[:, head]
        prob_grad = jnp.einsum(
            "tgd,sd->gts", head_grad, value_all[:, head], preferred_element_type=jnp.float32
        )
        score_grad = (
            probs * (prob_grad - jnp.sum(probs * prob_grad, axis=-1, keepdims=True))
        ).astype(jnp.bfloat16)
        value_heads.append(
            jnp.einsum(
                "gts,tgd->sd",
                probs.astype(jnp.bfloat16),
                head_grad,
                preferred_element_type=jnp.float32,
            )
        )
        key_heads.append(
            jnp.einsum(
                "gts,tgd->sd", score_grad, grouped[:, head], preferred_element_type=jnp.float32
            )
            * scale
        )
        query_heads.append(
            jnp.einsum(
                "gts,sd->tgd", score_grad, key_all[:, head], preferred_element_type=jnp.float32
            )
            * scale
        )
    query_grad = jnp.stack(query_heads, axis=1)
    key_all_grad = jnp.stack(key_heads, axis=1)
    value_all_grad = jnp.stack(value_heads, axis=1)
    key_back, value_back = (
        lax.psum_scatter(
            key_all_grad.reshape(-1, KVH * HD), "group", scatter_dimension=0, tiled=True
        ),
        lax.psum_scatter(
            value_all_grad.reshape(-1, KVH * HD), "group", scatter_dimension=0, tiled=True
        ),
    )
    query_pre_grad = (
        unrotate(query_grad.reshape(rows, H, HD), cosine, sine)
        .reshape(rows, H * HD)
        .astype(jnp.bfloat16)
    )
    key_pre_grad = (
        unrotate(key_back.reshape(rows, KVH, HD), cosine, sine)
        .reshape(rows, KVH * HD)
        .astype(jnp.bfloat16)
    )
    value_pre_grad = value_back.astype(jnp.bfloat16)
    query_wgrad = jnp.einsum(
        "tc,tq->cq", hidden_one, query_pre_grad, preferred_element_type=jnp.float32
    )
    key_wgrad = jnp.einsum(
        "tc,tq->cq", hidden_one, key_pre_grad, preferred_element_type=jnp.float32
    )
    value_wgrad = jnp.einsum(
        "tc,tq->cq", hidden_one, value_pre_grad, preferred_element_type=jnp.float32
    )
    query_bgrad = jnp.sum(query_pre_grad.astype(jnp.float32), axis=0)
    key_bgrad = jnp.sum(key_pre_grad.astype(jnp.float32), axis=0)
    value_bgrad = jnp.sum(value_pre_grad.astype(jnp.float32), axis=0)
    hidden_one_grad = jnp.einsum(
        "tq,cq->tc", query_pre_grad, query_mat, preferred_element_type=jnp.float32
    )
    hidden_one_grad = hidden_one_grad + jnp.einsum(
        "tq,cq->tc", key_pre_grad, key_mat, preferred_element_type=jnp.float32
    )
    hidden_one_grad = hidden_one_grad + jnp.einsum(
        "tq,cq->tc", value_pre_grad, value_mat, preferred_element_type=jnp.float32
    )
    gain_one_grad, through_one = norm_back(hidden_one_grad, normed_one, inv_one, gain_one)
    input_grad = middle_grad + through_one
    all_parts = (
        lax.psum_scatter(gain_one_grad, "group", scatter_dimension=0, tiled=True),
        lax.psum_scatter(query_wgrad, "group", scatter_dimension=0, tiled=True),
        lax.psum_scatter(query_bgrad, "group", scatter_dimension=0, tiled=True),
        lax.psum_scatter(key_wgrad, "group", scatter_dimension=0, tiled=True),
        lax.psum_scatter(key_bgrad, "group", scatter_dimension=0, tiled=True),
        lax.psum_scatter(value_wgrad, "group", scatter_dimension=0, tiled=True),
        lax.psum_scatter(value_bgrad, "group", scatter_dimension=0, tiled=True),
        lax.psum_scatter(out_wgrad, "group", scatter_dimension=0, tiled=True),
        lax.psum_scatter(gain_two_grad, "group", scatter_dimension=0, tiled=True),
        lax.psum_scatter(gate_wgrad, "group", scatter_dimension=0, tiled=True),
        lax.psum_scatter(up_wgrad, "group", scatter_dimension=0, tiled=True),
        lax.psum_scatter(down_grad, "group", scatter_dimension=0, tiled=True),
    )
    finished = lax.psum(
        (
            all_parts[0],
            all_parts[1],
            all_parts[2],
            all_parts[3],
            all_parts[4],
            all_parts[5],
            all_parts[6],
            all_parts[7],
            all_parts[8],
            all_parts[9],
            all_parts[10],
            all_parts[11],
        ),
        "replica",
    )
    return (
        block_output,
        input_grad,
        finished[0],
        finished[1],
        finished[2],
        finished[3],
        finished[4],
        finished[5],
        finished[6],
        finished[7],
        finished[8],
        finished[9],
        finished[10],
        finished[11],
    )


def solution(mesh):
    return jax.shard_map(
        local,
        mesh=mesh,
        in_specs=(
            P(("replica", "group"), None),
            P(("replica", "group"), None),
            P("group"),
            P("group", None),
            P("group"),
            P("group", None),
            P("group"),
            P("group", None),
            P("group"),
            P("group", None),
            P("group"),
            P("group", None),
            P("group", None),
            P("group", None),
        ),
        out_specs=(
            P(("replica", "group"), None),
            P(("replica", "group"), None),
            P("group"),
            P("group", None),
            P("group"),
            P("group", None),
            P("group"),
            P("group", None),
            P("group"),
            P("group", None),
            P("group"),
            P("group", None),
            P("group", None),
            P("group", None),
        ),
        check_vma=False,
    )
```

profile of v0, /device:TPU:0, one launch (start us, length us, event | category | flops | bytes accessed | tf_op | source)
XLA Modules:
  0.0 1355.7 jit_solution(424810566869754103)
XLA Ops:
  13.9 2.6 all-reduce.13
  27.2 2.6 all_gather.54
  30.0 4.8 convolution_add_fusion
  34.8 2.2 copy.56
  38.7 17.5 %fusion.74 = (f32[7,768]{1,0:T(8,128)S(1)}, f32[7,768,1536]{1,2,0:T(8,128)}) fusion(bf16[768,2,7,64]{0,3,2,1:T(8,128)(2,1)S(1)} %fusion.29, bf16[1536,2,64]{0,2,1:T(8,128)(2,1)S(1)} %bitcast.221, pred[768,1536]{0,1:T(8,128)(4,1)S(1)} %copy-done.43), kind=kOutput, calls=%fused_computation.133 | convolution fusion | flops 1081731840 | bytes 35116032 | tf_op jit(solution)/shard_map/tgd,sd->gts/dot_general | solution.py:127
  56.1 15.0 %fusion.75 = (f32[7,768]{1,0:T(8,128)S(1)}, f32[7,768,1536]{1,2,0:T(8,128)}) fusion(bf16[768,2,7,64]{0,3,2,1:T(8,128)(2,1)S(1)} %fusion.29, bf16[1536,2,64]{0,2,1:T(8,128)(2,1)S(1)} %bitcast.222, pred[768,1536]{0,1:T(8,128)(4,1)S(1)} %copy-done.43), kind=kOutput, calls=%fused_computation.134 | convolution fusion | flops 1081731840 | bytes 35116032 | tf_op jit(solution)/shard_map/tgd,sd->gts/dot_general | solution.py:127
  71.2 15.1 %exponential_reduce_fusion = f32[7,768]{1,0:T(8,128)S(1)} fusion(f32[7,768,1536]{1,2,0:T(8,128)} %get-tuple-element.58, f32[7,768]{1,0:T(8,128)S(1)} %get-tuple-element.57), kind=kLoop, calls=%fused_computation.13 | loop fusion | flops 16509696 | bytes 33073152 | tf_op jit(solution)/shard_map/reduce_sum | solution.py:142
  86.3 9.2 copy-done
  95.4 4.5 exponential_reduce_fusion.1
  100.0 13.2 fusion.50
  113.3 13.4 fusion.53
  128.5 3.5 multiply_reduce_fusion.2
  133.9 14.6 %fusion.76 = f32[768,4864]{1,0:T(8,128)} fusion(bf16[768,896]{1,0:T(8,128)(2,1)S(1)} %multiply_convert_fusion.3, bf16[896,4864]{1,0:T(8,128)(2,1)} %all-gather.10.cloned.1.call-done), kind=kOutput, calls=%fused_computation.135 | convolution fusion | flops 6694109184 | bytes 25034752 | tf_op jit(solution)/shard_map/dot_general | solution.py:159
  148.5 14.1 %fusion.77 = f32[768,4864]{1,0:T(8,128)} fusion(bf16[768,896]{1,0:T(8,128)(2,1)S(1)} %multiply_convert_fusion.3, bf16[896,4864]{1,0:T(8,128)(2,1)} %all-gather.12.cloned.1.call-done), kind=kOutput, calls=%fused_computation.136 | convolution fusion | flops 6694109184 | bytes 25034752 | tf_op jit(solution)/shard_map/dot_general | solution.py:160
  162.5 24.6 %multiply_convert_fusion = (bf16[768,4864]{1,0:T(8,128)(2,1)}, bf16[768,4864]{1,0:T(8,128)(2,1)}, bf16[768,4864]{1,0:T(8,128)(2,1)}) fusion(f32[768,4864]{1,0:T(8,128)} %fusion.76, f32[768,4864]{1,0:T(8,128)} %fusion.77, bf16[768,896]{1,0:T(8,128)(2,1)S(1)} %copy-done.38, bf16[4864,896]{1,0:T(8,128)(2,1)} %all-gather.14.cloned.1.call-done), kind=kOutput, calls=%fused_computation.18 | convolution fusion | flops 6750142464 | bytes 62390272 | tf_op jit(solution)/shard_map/td,fd->tf/dot_general | solution.py:180
  187.1 14.2 %fusion.78 = f32[768,896]{1,0:T(8,128)} fusion(bf16[768,4864]{1,0:T(8,128)(2,1)} %get-tuple-element.43, bf16[896,4864]{1,0:T(8,128)(2,1)} %all-gather.10.cloned.1.call-done), kind=kOutput, calls=%fused_computation.137 | convolution fusion | flops 6694109184 | bytes 18939904 | tf_op jit(solution)/shard_map/tf,cf->tc/dot_general | solution.py:187
  201.3 13.2 multiply_reduce_fusion
  214.5 2.6 multiply_add_fusion
  221.3 13.1 fusion.35
  234.5 25.1 %fusion = (f32[7,768]{1,0:T(8,128)}, f32[1536,768,7]{1,0,2:T(8,128)}) fusion(f32[7,768,1536]{1,2,0:T(8,128)} %get-tuple-element.58, f32[7,768]{1,0:T(8,128)S(1)} %log_add_fusion, bf16[768,2,7,64]{0,3,2,1:T(8,128)(2,1)S(1)} %bitcast.203, bf16[1536,2,64]{0,2,1:T(8,128)(2,1)S(1)} %bitcast.214), kind=kOutput, calls=%fused_computation.2 | convolution fusion | flops 1081731840 | bytes 66991104 | tf_op jit(solution)/shard_map/tgd,sd->gts/dot_general | solution.py:210
  259.5 25.4 %fusion.3 = (f32[7,768]{1,0:T(8,128)}, f32[1536,768,7]{1,0,2:T(8,128)}) fusion(f32[7,768,1536]{1,2,0:T(8,128)} %get-tuple-element.60, f32[7,768]{1,0:T(8,128)S(1)} %copy-done.31, bf16[768,2,7,64]{0,3,2,1:T(8,128)(2,1)S(1)} %bitcast.204, bf16[1536,2,64]{0,2,1:T(8,128)(2,1)S(1)} %bitcast.215), kind=kOutput, calls=%fused_computation.7 | convolution fusion | flops 1081731840 | bytes 66991104 | tf_op jit(solution)/shard_map/tgd,sd->gts/dot_general | solution.py:210
  284.9 27.9 %fusion.2 = bf16[7,768,1536]{1,2,0:T(8,128)(2,1)} fusion(f32[1536,768,7]{1,0,2:T(8,128)} %get-tuple-element.65, f32[7,768,1536]{1,2,0:T(8,128)} %get-tuple-element.58, f32[7,768]{1,0:T(8,128)} %get-tuple-element.64, f32[7,768]{1,0:T(8,128)} %copy-done.33), kind=kLoop, calls=%fused_computation.4 | loop fusion | flops 33030144 | bytes 82618368 | tf_op jit(solution)/shard_map/convert_element_type | solution.py:215
  312.8 11.5 fusion.39
  324.3 27.6 %fusion.5 = bf16[7,768,1536]{1,2,0:T(8,128)(2,1)} fusion(f32[1536,768,7]{1,0,2:T(8,128)} %get-tuple-element.67, f32[7,768,1536]{1,2,0:T(8,128)} %get-tuple-element.60, f32[7,768]{1,0:T(8,128)S(1)} %copy-done.48, f32[7,768]{1,0:T(8,128)S(1)} %copy-done.32), kind=kLoop, calls=%fused_computation.9 | loop fusion | flops 33030144 | bytes 82618368 | tf_op jit(solution)/shard_map/convert_element_type | solution.py:215
  352.0 10.8 fusion.41
  363.8 13.3 fusion.32
  378.3 8.8 fusion.42
  390.7 8.8 fusion.43
  402.4 2.4 fusion.67
  411.4 3.4 fusion.81
  416.2 5.1 fusion.57
  422.6 13.0 fusion.83
  435.6 13.0 fusion.84
  450.0 17.6 %fusion.85 = f32[4864,896]{1,0:T(8,128)} fusion(bf16[768,4864]{1,0:T(8,128)(2,1)} %get-tuple-element.44, bf16[768,896]{1,0:T(8,128)(2,1)S(1)} %copy-done.39), kind=kOutput, calls=%fused_computation.144 | convolution fusion | flops 6694109184 | bytes 26279936 | tf_op jit(solution)/shard_map/tf,td->fd/dot_general | solution.py:179
  468.1 7.0 reduce-scatter.22.cloned.1.call-done
  475.1 30.4 %reduce-scatter.24.cloned.1.call-done = f32[448,4864]{1,0:T(8,128)} async-done(((f32[896,4864]{1,0:T(8,128)}), f32[448,4864]{1,0:T(8,128)}) %reduce-scatter.24.cloned.1.call-update) | async-done | bytes 8716304 | tf_op jit(solution)/shard_map/reduce_scatter | solution.py:292
  505.5 30.2 %reduce-scatter.26.cloned.1.call-done = f32[2432,896]{1,0:T(8,128)} async-done(((f32[4864,896]{1,0:T(8,128)}), f32[2432,896]{1,0:T(8,128)}) %reduce-scatter.26.cloned.1.call-update) | async-done | bytes 8716304 | tf_op jit(solution)/shard_map/reduce_scatter | solution.py:293
  539.3 3.8 fusion.79
  543.1 13.6 %add_convert_fusion = bf16[768,896]{1,0:T(8,128)(2,1)} fusion(f32[768,896]{1,0:T(8,128)S(1)} %copy-done.17, bf16[768,4864]{1,0:T(8,128)(2,1)} %get-tuple-element.44, bf16[4864,896]{1,0:T(8,128)(2,1)} %all-gather.14.cloned.1.call-done), kind=kOutput, calls=%fused_computation.58 | convolution fusion | flops 6695485440 | bytes 20316160 | tf_op jit(solution)/shard_map/dot_general | solution.py:164
  558.1 2.9 fusion.26
  561.0 3.4 all-reduce.12
  564.7 45.7 %all-reduce.10 = (f32[448]{0:T(512)}, f32[448]{0:T(512)}, f32[64]{0:T(128)}, f32[64]{0:T(128)}, f32[448]{0:T(512)}) all-reduce(f32[448]{0:T(512)S(1)} %dynamic-slice.6, f32[448]{0:T(512)S(1)} %dynamic-slice.8, f32[64]{0:T(128)S(1)} %dynamic-slice.10, f32[64]{0:T(128)S(1)} %dynamic-slice.12, ...), channel_id=1, replica_groups=mesh['replica'=16,'group'=2] {'replica'}, use_global_device_ids=true, to_apply=%region_14.15 | all-reduce | flops 1472 | bytes 11776 | tf_op jit(solution)/shard_map/psum | solution.py:295
  610.4 4.9 fusion.25
  615.3 710.0 %all-reduce.16.cloned.1.call-done = (f32[448,896]{1,0:T(8,128)}, f32[448,128]{1,0:T(8,128)}, f32[448,128]{1,0:T(8,128)}, f32[448,896]{1,0:T(8,128)}, f32[448,486...) async-done(((f32[448,896]{1,0:T(8,128)}, f32[448,128]{1,0:T(8,128)}, f32[448,128]{1,0:T(8,128)}, f32[448,896]{1,0:T(8,128)}, f32[448,4864]{1,0:T(8,128)}, ...) | async-done | bytes 29818896 | tf_op jit(solution)/shard_map/psum | solution.py:295
  1325.3 2.8 copy.87
  1330.7 8.6 copy.91
  1339.3 4.4 copy.92
  1345.4 3.5 copy.93
  (239 shorter events, 53.2 us)
Async XLA Ops:
  7.2 22.8 %all-gather.6.cloned.1.call-start = ((), (), s32[]{:S(2)}) async-start(), calls=%async_computation.9 | async-start | bytes 2408448 | tf_op jit(solution)/shard_map/all_gather | solution.py:66
  7.9 118.9 %all-gather.8.cloned.1.call-start = ((), (), s32[]{:S(2)}) async-start(), calls=%async_computation.10 | async-start | bytes 2408448 | tf_op jit(solution)/shard_map/all_gather | solution.py:72
  8.7 125.3 %all-gather.10.cloned.1.call-start = ((), (), s32[]{:S(2)}) async-start(), calls=%async_computation.11 | async-start | bytes 13074432 | tf_op jit(solution)/shard_map/all_gather | solution.py:74
  9.4 139.1 %all-gather.12.cloned.1.call-start = ((), (), s32[]{:S(2)}) async-start(), calls=%async_computation.12 | async-start | bytes 13074432 | tf_op jit(solution)/shard_map/all_gather | solution.py:75
  10.0 6.5 copy-start.7
  10.1 7.3 copy-start.46
  10.1 152.5 %all-gather.14.cloned.1.call-start = ((), (), s32[]{:S(2)}) async-start(), calls=%async_computation.13 | async-start | bytes 13074432 | tf_op jit(solution)/shard_map/all_gather | solution.py:76
  10.6 376.5 %reduce-scatter.10.cloned.1.call-start = ((), (), s32[]{:S(2)}) async-start(), calls=%async_computation.14 | async-start | bytes 1179648 | tf_op jit(solution)/shard_map/reduce_scatter | solution.py:240
  16.5 3.9 copy-start.49
  17.3 19.9 %copy-start.23 = (f32[768,64]{0,1:T(8,128)}, f32[768,64]{0,1:T(8,128)S(1)}, u32[]{:S(2)}) copy-start(f32[768,64]{0,1:T(8,128)S(1)} %pad_maximum_fusion.7) | copy-start | bytes 589828
  17.4 19.9 %copy-start.19 = (f32[768,64]{0,1:T(8,128)}, f32[768,64]{0,1:T(8,128)S(1)}, u32[]{:S(2)}) copy-start(f32[768,64]{0,1:T(8,128)S(1)} %pad_maximum_fusion.6) | copy-start | bytes 589828
  19.7 10.3 copy-start.1
  20.4 4.3 copy-start.47
  37.8 18.3 %copy-start.21 = (bf16[768,2,7,64]{0,3,2,1:T(8,128)(2,1)}, bf16[768,2,7,64]{0,3,2,1:T(8,128)(2,1)S(1)}, u32[]{:S(2)}) copy-start(bf16[768,2,7,64]{0,3,2,1:T(8,128)(2,1)S(1)} %fusion.29) | copy-start | bytes 4128772
  71.2 24.3 %copy-start = (f32[7,768,1536]{1,2,0:T(8,128)S(1)}, f32[7,768,1536]{1,2,0:T(8,128)}, u32[]{:S(2)}) copy-start(f32[7,768,1536]{1,2,0:T(8,128)} %get-tuple-element.60) | copy-start | bytes 99090432
  86.3 148.2 %copy-start.33 = (f32[7,768]{1,0:T(8,128)}, f32[7,768]{1,0:T(8,128)S(1)}, u32[]{:S(2)}) copy-start(f32[7,768]{1,0:T(8,128)S(1)} %log_add_fusion) | copy-start | bytes 64516
  100.0 13.3 copy-start.30
  126.8 5.2 copy-start.41
  133.9 14.6 %copy-start.3 = (bf16[768,896]{1,0:T(8,128)(2,1)}, bf16[768,896]{1,0:T(8,128)(2,1)S(1)}, u32[]{:S(2)}) copy-start(bf16[768,896]{1,0:T(8,128)(2,1)S(1)} %multiply_convert_fusion.3) | copy-start | bytes 4128772
  148.5 14.1 %copy-start.38 = (bf16[768,896]{1,0:T(8,128)(2,1)S(1)}, bf16[768,896]{1,0:T(8,128)(2,1)}, u32[]{:S(2)}) copy-start(bf16[768,896]{1,0:T(8,128)(2,1)} %param.15) | copy-start | bytes 4128772
  187.1 14.2 %copy-start.5 = (bf16[768,4864]{1,0:T(8,128)(2,1)S(1)}, bf16[768,4864]{1,0:T(8,128)(2,1)}, u32[]{:S(2)}) copy-start(bf16[768,4864]{1,0:T(8,128)(2,1)} %get-tuple-element.42) | copy-start | bytes 22413316
  187.1 14.2 %copy-start.16 = (f32[768,896]{1,0:T(8,128)S(1)}, f32[768,896]{1,0:T(8,128)}, u32[]{:S(2)}) copy-start(f32[768,896]{1,0:T(8,128)} %copy-done.15) | copy-start | bytes 8257540
  214.5 4.2 copy-start.58
  234.4 25.1 %copy-start.31 = (f32[7,768]{1,0:T(8,128)S(1)}, f32[7,768]{1,0:T(8,128)}, u32[]{:S(2)}) copy-start(f32[7,768]{1,0:T(8,128)} %copy-done.30) | copy-start | bytes 64516
  284.9 27.9 %copy-start.22 = (bf16[768,2,7,64]{0,3,2,1:T(8,128)(2,1)S(1)}, bf16[768,2,7,64]{0,3,2,1:T(8,128)(2,1)}, u32[]{:S(2)}) copy-start(bf16[768,2,7,64]{0,3,2,1:T(8,128)(2,1)} %copy-done.21) | copy-start | bytes 4128772
  312.8 11.5 copy-start.32
  312.8 11.5 copy-start.48
  352.0 10.8 copy-start.37
  363.8 38.7 %reduce-scatter.12.cloned.1.call-start = ((), (), s32[]{:S(2)}) async-start(), calls=%async_computation.15 | async-start | bytes 1179648 | tf_op jit(solution)/shard_map/reduce_scatter | solution.py:243
  378.1 9.1 copy-start.24
  378.1 10.7 copy-start.20
  378.1 89.9 %reduce-scatter.16.cloned.1.call-start = ((), (), s32[]{:S(2)}) async-start(), calls=%async_computation.17 | async-start | bytes 688128 | tf_op jit(solution)/shard_map/reduce_scatter | solution.py:285
  387.1 12.3 copy-start.12
  390.6 77.4 %reduce-scatter.18.cloned.1.call-start = ((), (), s32[]{:S(2)}) async-start(), calls=%async_computation.18 | async-start | bytes 688128 | tf_op jit(solution)/shard_map/reduce_scatter | solution.py:287
  404.8 63.3 %reduce-scatter.14.cloned.1.call-start = ((), (), s32[]{:S(2)}) async-start(), calls=%async_computation.16 | async-start | bytes 4816896 | tf_op jit(solution)/shard_map/reduce_scatter | solution.py:283
  414.8 53.3 %reduce-scatter.20.cloned.1.call-start = ((), (), s32[]{:S(2)}) async-start(), calls=%async_computation.19 | async-start | bytes 4816896 | tf_op jit(solution)/shard_map/reduce_scatter | solution.py:289
  421.2 53.8 %reduce-scatter.22.cloned.1.call-start = ((), (), s32[]{:S(2)}) async-start(), calls=%async_computation.20 | async-start | bytes 26148864 | tf_op jit(solution)/shard_map/reduce_scatter | solution.py:291
  435.6 69.9 %reduce-scatter.24.cloned.1.call-start = ((), (), s32[]{:S(2)}) async-start(), calls=%async_computation.21 | async-start | bytes 26148864 | tf_op jit(solution)/shard_map/reduce_scatter | solution.py:292
  448.7 87.0 %reduce-scatter.26.cloned.1.call-start = ((), (), s32[]{:S(2)}) async-start(), calls=%async_computation.22 | async-start | bytes 26148864 | tf_op jit(solution)/shard_map/reduce_scatter | solution.py:293
  467.7 857.6 %all-reduce.16.cloned.1.call-start = ((), (), s32[]{:S(2)}) async-start(), calls=%async_computation.23 | async-start | bytes 59637760 | tf_op jit(solution)/shard_map/psum | solution.py:295
  539.3 3.8 copy-start.17
  543.1 13.7 %copy-start.25 = (f32[768,128]{0,1:T(8,128)S(1)}, f32[768,128]{0,1:T(8,128)}, u32[]{:S(2)}) copy-start(f32[768,128]{0,1:T(8,128)} %reduce-scatter.12.cloned.1.call-done) | copy-start | bytes 1179652
  543.1 13.8 %copy-start.27 = (bf16[896,128]{1,0:T(8,128)(2,1)S(1)}, bf16[896,128]{1,0:T(8,128)(2,1)}, u32[]{:S(2)}) copy-start(bf16[896,128]{1,0:T(8,128)(2,1)} %copy-done.26) | copy-start | bytes 688132
  1325.3 4.2 copy-start.34
  1330.6 8.6 copy-start.18
  1330.6 13.0 slice-start
  1330.7 14.6 %slice-start.1 = ((s8[8716288]{0:T(1024)(128)(4,1)}), s8[4194304]{0:T(1024)(128)(4,1)S(1)}, s32[]{:S(2)}) async-start(s8[8716288]{0:T(1024)(128)(4,1)} %bitcast.208), calls=%async_computation.25 | async-start | bytes 8388608
  1339.3 6.1 slice-start.2
  (31 other events, 60.8 us)
Sparse Core Ops, SparseCore 0:
  9.6 12.5 all-gather.5
  23.7 11.0 all-gather.7
  36.3 22.1 all-gather.9
  59.9 22.1 all-gather.11
  83.5 22.1 all-gather.13
  363.9 11.4 reduce-scatter.9
  378.3 11.5 reduce-scatter.11
  392.1 9.7 reduce-scatter.15
  404.9 11.1 reduce-scatter.17
  418.3 12.1 reduce-scatter.13
  432.8 12.1 reduce-scatter.19
  447.1 27.9 reduce-scatter.21
  477.5 27.9 reduce-scatter.23
  507.7 27.9 reduce-scatter.25
  543.1 782.1 all-reduce.15
where the time goes:
time: 1360 us
  waiting for transfers between devices  781 us (57%)
  matrix products  344 us (25%)
  other arithmetic  97.6 us (7%)
  blocking collectives  60.3 us (4%)
  local copies, waits for them, and re-layouts  53.3 us (4%)
  between operations  17.8 us (1%)
    psum x1, waiting for transfers between devices, local(): lax.psum((all_parts[0], all_parts[1], all_parts[2], all_parts[3], all_par...  710 us
    convert_element_type x2, other arithmetic, local(): score_grad = (probs * (prob_grad - jnp.sum(probs * prob_grad, axis=-1, ke...  55.6 us
    dot_general x2, matrix products, local(): jnp.einsum('tgd,sd->gts', head_grad, value_all[:, head], preferred_elemen...  50.4 us
    unnamed x151, local copies, waits for them, and re-layouts  50 us
    psum x1, blocking collectives, local(): lax.psum((all_parts[0], all_parts[1], all_parts[2], all_parts[3], all_par...  45.7 us
    dot_general x2, matrix products, scores_of(): jnp.einsum('tgd,sd->gts', grouped[:, head], key_all[:, head], preferred_e...  32.5 us
    reduce_scatter x1, waiting for transfers between devices, local(): lax.psum_scatter(up_wgrad, 'group', scatter_dimension=0, tiled=True)  30.4 us
    reduce_scatter x1, waiting for transfers between devices, local(): lax.psum_scatter(down_grad, 'group', scatter_dimension=0, tiled=True)  30.2 us
  transfers between devices with their start and end apart: 15, of which 4 were waited for; matrix products, arithmetic and copies ran while one was open for 18% of the time, Pallas kernels for 0%

commit v1 on v0

v1 whole, which is shorter than its diff:
```python
import functools
import math

import jax
import jax.numpy as jnp
import numpy as np
from jax import lax
from jax.experimental import pallas as pl
from jax.experimental.pallas import tpu as pltpu
from jax.sharding import PartitionSpec as P

H = 14
KVH = 2
HD = 64


norm_eps = 1e-06
rope_base = 1000000.0
masked_score = -1e30


MESH = pl.DeviceIdType.MESH
LANES = 128
ROWS = 1344
HALF = ROWS // 2
QUARTER = ROWS // 4


class Ladder:
    STAGES = ("split", "inward", "middle", "last", "share", "outward", "join")

    def __init__(self, chunks, length, acc, split, inward, middle, last, send, recv, freed, done):
        self.chunks, self.length = chunks, length
        self.levels = length // 2 - 1
        self.slots = self.slots_of(length)
        self.acc = acc
        self.landing = {"split": split, "inward": inward, "middle": middle, "last": last}
        self.send, self.recv, self.freed, self.done = send, recv, freed, done
        me = lax.axis_index("replica")
        x, y, z = lax.rem(me, 2), lax.rem(lax.div(me, 2), 2), lax.div(me, 4)
        low = z < length // 2
        self.depth = jnp.where(low, z, length - 1 - z)
        self.across_x, self.across_y = me + 1 - 2 * x, me + 2 - 4 * y
        self.inner = jnp.where(low, me + 4, me - 4)
        self.outer = jnp.where(low, me - 4, me + 4)
        self.first_bit = (x, y)
        self.first = (self.across_x, self.across_y)
        self.second = (self.across_y, self.across_x)
        self.mid_bit = jnp.where(low, 0, 1)

    @staticmethod
    def slots_of(length):
        return 4 + length // 2

    def neighbours(self):
        return [self.across_x, self.across_y, self.inner]

    def rows(self, lot, kind):
        bit = self.first_bit[lot]
        mine = bit * HALF
        if kind == "other half":
            return pl.ds(pl.multiple_of((1 - bit) * HALF, 16), HALF)
        if kind == "half":
            return pl.ds(pl.multiple_of(mine, 16), HALF)
        if kind == "other quarter":
            return pl.ds(pl.multiple_of(mine + (1 - self.mid_bit) * QUARTER, 16), QUARTER)
        return pl.ds(pl.multiple_of(mine + self.mid_bit * QUARTER, 16), QUARTER)

    def berth(self, stage, chunk):
        return lax.rem(chunk, self.landing[stage].shape[0])

    def copy(self, stage, chunk, lot):
        slot = lax.rem(chunk, self.slots)
        kind = {
            "split": "other half",
            "inward": "half",
            "middle": "other quarter",
            "last": "quarter",
            "share": "quarter",
            "outward": "half",
            "join": "half",
        }[stage]
        target = {
            "split": self.first[lot],
            "inward": self.inner,
            "middle": self.inner,
            "last": self.second[lot],
            "share": self.inner,
            "outward": self.outer,
            "join": self.first[lot],
        }[stage]
        source = self.acc.at[chunk, lot, self.rows(lot, kind)]
        goal = self.landing[stage].at[self.berth(stage, chunk), lot] if stage in self.landing else source
        row = self.STAGES.index(stage)
        return pltpu.make_async_remote_copy(
            src_ref=source,
            dst_ref=goal,
            send_sem=self.send.at[row, slot, lot],
            recv_sem=self.recv.at[row, slot, lot],
            device_id={"replica": target},
            device_id_type=MESH,
        )

    def add(self, stage, chunk, lot, kind):
        rows = self.rows(lot, kind)
        mine = self.acc[chunk, lot, rows].astype(jnp.float32)
        theirs = self.landing[stage][self.berth(stage, chunk), lot].astype(jnp.float32)
        self.acc[chunk, lot, rows] = (mine + theirs).astype(jnp.bfloat16)

    def start(self, stage, chunk):
        for lot in (0, 1):
            self.copy(stage, chunk, lot).start()

    def at(self, time, offset, depth, body):
        chunk = time - offset
        live = (chunk >= 0) & (chunk < self.chunks)
        if depth is not None:
            live = live & (self.depth == depth)
        pl.when(live)(functools.partial(body, chunk))

    def free(self, stage, lot):
        target = self.first[lot] if stage == "split" else self.inner
        row = self.STAGES.index(stage)
        pl.semaphore_signal(
            self.freed.at[row, lot], inc=1, device_id={"replica": target}, device_id_type=MESH
        )

    def wait_free(self, stage):
        for lot in (0, 1):
            pl.semaphore_wait(self.freed.at[self.STAGES.index(stage), lot], 1)

    def take(self, stage, kind, chunk):
        for lot in (0, 1):
            copy = self.copy(stage, chunk, lot)
            if stage != "inward":
                copy.wait_send()
            if stage in ("split", "middle"):
                self.free(stage, lot)
            copy.wait_recv()
            self.add(stage, chunk, lot, kind)

    def tick(self, time):
        deep = self.levels

        def split(chunk):
            self.start("split", chunk)

        def halves(chunk):
            self.take("split", "half", chunk)

        def pass_on(level, chunk):
            if level:
                self.take("inward", "half", chunk)
            self.start("inward" if level < deep else "middle", chunk)

        def sent_inward(chunk):
            for lot in (0, 1):
                self.copy("inward", chunk, lot).wait_send()
                self.free("inward", lot)

        def quarters(chunk):
            self.take("middle", "quarter", chunk)
            self.start("last", chunk)

        def finish(chunk):
            self.take("last", "quarter", chunk)
            self.wait_free("middle")
            self.start("share", chunk)

        def shared(chunk):
            for lot in (0, 1):
                self.copy("share", chunk, lot).wait()
            if deep:
                self.wait_free("inward")
                self.start("outward", chunk)
            self.wait_free("split")
            self.start("join", chunk)

        def back(level, chunk):
            for lot in (0, 1):
                self.copy("outward", chunk, lot).wait_recv()
            if level:
                self.wait_free("inward")
                self.start("outward", chunk)
            self.wait_free("split")
            self.start("join", chunk)

        def joined(level, chunk):
            for lot in (0, 1):
                self.copy("join", chunk, lot).wait()
                if level:
                    self.copy("outward", chunk, lot).wait_send()
            self.done(chunk)

        self.at(time, 1, None, split)
        self.at(time, 2, None, halves)
        for level in range(deep + 1):
            self.at(time, 2 + level, level, functools.partial(pass_on, level))
        for level in range(deep):
            self.at(time, 3 + level, level, sent_inward)
        self.at(time, 3 + deep, deep, quarters)
        self.at(time, 4 + deep, deep, finish)
        self.at(time, 5 + deep, deep, shared)
        for level in range(deep - 1, -1, -1):
            self.at(time, 5 + 2 * deep - level, level, functools.partial(back, level))
        for level in range(deep, -1, -1):
            self.at(time, 6 + 2 * deep - level, level, functools.partial(joined, level))


def last_offset(length):
    return 6 + 2 * (length // 2 - 1)


def enter(ladder, partner):
    barrier = pltpu.get_barrier_semaphore()
    for neighbour in ladder.neighbours():
        pl.semaphore_signal(barrier, inc=1, device_id={"replica": neighbour}, device_id_type=MESH)
    pl.semaphore_signal(barrier, inc=1, device_id={"group": partner}, device_id_type=MESH)
    outside = ladder.depth > 0

    @pl.when(outside)
    def _():
        pl.semaphore_signal(barrier, inc=1, device_id={"replica": ladder.outer}, device_id_type=MESH)

    pl.semaphore_wait(barrier, jnp.where(outside, 5, 4))


BLOCK = 256


def dot(left, right):
    return jnp.dot(left, right, preferred_element_type=jnp.float32)


def dot_nt(left, right):
    return lax.dot_general(left, right, (((1,), (1,)), ((), ())), preferred_element_type=jnp.float32)


def tables(positions, width):
    half = width // 2
    freqs = np.float32(rope_base) ** (-(np.arange(half, dtype=np.float32) * np.float32(2.0 / width)))
    angles = freqs[:, None] * np.arange(positions, dtype=np.float32)[None, :]
    return np.stack([np.cos(angles), np.sin(angles)]).astype(np.float32)


def turn(head, cosine, sine):
    top, low = head[: HD // 2], head[HD // 2 :]
    return jnp.concatenate([top * cosine - low * sine, low * cosine + top * sine], axis=0)


def turn_back(head, cosine, sine):
    top, low = head[: HD // 2], head[HD // 2 :]
    return jnp.concatenate([top * cosine + low * sine, low * cosine - top * sine], axis=0)


def span(number, size):
    return pl.ds(pl.multiple_of(number * size, size), size)


def front_kernel(
    tokens,
    first_gain,
    query_bias,
    key_bias,
    value_bias,
    second_gain,
    angle_hbm,
    query_hbm,
    key_hbm,
    value_hbm,
    out_hbm,
    gate_hbm,
    up_hbm,
    down_hbm,
    hidden_two,
    middle,
    turned_one,
    queries,
    keys,
    values,
    keys_turned,
    attended_turned,
    attended_rest,
    log_totals,
    vectors_full,
    query_full,
    key_full,
    value_full,
    out_full,
    gate_other,
    up_other,
    down_other,
    query_mat,
    key_mat,
    value_mat,
    out_mat,
    vectors,
    vectors_other,
    angles,
    hidden,
    wide,
    values_turned,
    own_pair,
    far_pair,
    scores,
    tops,
    totals,
    attended,
    load,
    send,
    recv,
    store,
):
    rank = lax.axis_index("group")
    partner = 1 - rank
    rows, width = tokens.shape
    share = width // 2
    blocks = rows // BLOCK
    ratio = H // KVH
    low, f32 = jnp.bfloat16, jnp.float32

    barrier = pltpu.get_barrier_semaphore()
    pl.semaphore_signal(barrier, inc=1, device_id={"group": partner}, device_id_type=MESH)

    weights = ((key_hbm, key_mat), (value_hbm, value_mat), (query_hbm, query_mat), (out_hbm, out_mat))
    own_rows = pl.ds(pl.multiple_of(rank * share, 16), share)
    local = [
        pltpu.make_async_copy(source, goal.at[own_rows], load.at[number])
        for number, (source, goal) in enumerate(weights)
    ]
    table = pltpu.make_async_copy(angle_hbm.at[:, :, span(rank, rows)], angles, load.at[4])
    for copy in (table, *local):
        copy.start()

    def push(source, goal, number):
        return pltpu.make_async_remote_copy(
            src_ref=source,
            dst_ref=goal,
            send_sem=send.at[number],
            recv_sem=recv.at[number],
            device_id={"group": partner},
            device_id_type=MESH,
        )

    vectors[...] = jnp.zeros_like(vectors)
    for line, item in enumerate((first_gain, query_bias, key_bias, value_bias, second_gain)):
        vectors[line : line + 1, : item.shape[0]] = item[...].astype(f32).reshape(1, -1)
    pushes = [push(vectors, vectors_other, 4)]
    pushes += [push(source, goal.at[own_rows], number) for number, (source, goal) in enumerate(weights)]
    pushes += [
        push(source, goal, 5 + number)
        for number, (source, goal) in enumerate(
            ((gate_hbm, gate_other), (up_hbm, up_other), (down_hbm, down_other))
        )
    ]
    pair_push = push(own_pair, far_pair, 8)
    pl.semaphore_wait(barrier, 1)
    for copy in pushes:
        copy.start()

    pushes[0].wait_recv()
    first = jnp.where(rank == 0, vectors[...], vectors_other[...])
    second = jnp.where(rank == 0, vectors_other[...], vectors[...])
    vectors_full[...] = jnp.concatenate([first, second], axis=1)
    part = KVH * HD // 2
    vectors_full[2:4, : 2 * part] = jnp.concatenate([first[2:4, :part], second[2:4, :part]], axis=1)

    def norm_one(number, carry):
        at = span(number, BLOCK)
        residual = tokens[at].astype(f32)
        inverse = lax.rsqrt(jnp.mean(residual * residual, axis=-1, keepdims=True) + norm_eps)
        block = (residual * inverse * vectors_full[0:1]).astype(low)
        hidden[at] = block
        turned_one[:, at] = block.T
        return carry

    lax.fori_loop(0, blocks, norm_one, 0)

    table.wait()
    own_columns = span(rank, rows)
    for number, goal in ((1, keys), (2, values)):
        pushes[number].wait_recv()
        local[number - 1].wait()
        mat, bias_row = ((key_mat, 2), (value_mat, 3))[number - 1]
        raw = dot(hidden[...], mat[...]) + vectors_full[bias_row : bias_row + 1, : KVH * HD]
        if number == 1:
            turned = raw.T
            heads = [
                turn(turned[head * HD : (head + 1) * HD], angles[0], angles[1]).astype(low) for head in range(KVH)
            ]
            both = jnp.concatenate(heads, axis=0)
            keys_turned[:, own_columns] = both
            own_pair[0] = both.T
        else:
            own_pair[1] = raw.astype(low)
            values_turned[:, own_columns] = raw.T.astype(low)
        for head in range(KVH):
            goal[head, own_columns] = own_pair[number - 1, :, head * HD : (head + 1) * HD]

    @pl.when(rank == 0)
    def _():
        pair_push.start()

    pushes[3].wait_recv()
    local[2].wait()
    wide[...] = dot(hidden[...], query_mat[...])
    for pair in range(H // 2):
        columns = slice(pair * 2 * HD, (pair + 1) * 2 * HD)
        turned = (wide[:, columns] + vectors_full[1:2, columns]).T
        for inside in range(2):
            head = turn(turned[inside * HD : (inside + 1) * HD], angles[0], angles[1])
            head = (head.astype(low).astype(f32) * (1.0 / math.sqrt(HD))).astype(low)
            group, place = divmod(pair * 2 + inside, ratio)
            for block in range(blocks):
                queries[group * blocks + block, :, place * BLOCK : (place + 1) * BLOCK] = head[
                    :, block * BLOCK : (block + 1) * BLOCK
                ]

    @pl.when(rank == 1)
    def _():
        pair_push.wait_recv()
        keys_turned[:, :rows] = far_pair[0].T
        values_turned[:, :rows] = far_pair[1].T
        for head in range(KVH):
            keys[head, :rows] = far_pair[0, :, head * HD : (head + 1) * HD]
            values[head, :rows] = far_pair[1, :, head * HD : (head + 1) * HD]

    key_place = lax.broadcasted_iota(jnp.int32, (BLOCK, BLOCK), 0)
    query_place = lax.broadcasted_iota(jnp.int32, (BLOCK, BLOCK), 1)

    lanes = ratio * BLOCK
    query_place = jnp.concatenate([query_place] * ratio, axis=1)
    key_place = jnp.concatenate([key_place] * ratio, axis=1)

    def attend(index, carry):
        group, block = lax.div(index, blocks), lax.rem(index, blocks)
        tops[...] = jnp.full_like(tops, masked_score)
        totals[...] = jnp.zeros_like(totals)
        attended[...] = jnp.zeros_like(attended)
        diagonal = rank * blocks + block

        def score(number, masked):
            at = span(number, BLOCK)
            block_scores = dot(keys[group, at], queries[index])
            if masked:
                block_scores = jnp.where(key_place <= query_place, block_scores, masked_score)
            scores[number] = block_scores
            tops[...] = jnp.maximum(tops[...], jnp.max(block_scores.reshape(BLOCK // 8, 8, lanes), axis=0))

        def score_full(number, inner):
            score(number, False)
            return inner

        lax.fori_loop(0, diagonal, score_full, 0)
        score(diagonal, True)
        top = jnp.max(tops[...], axis=0, keepdims=True)

        def weigh(number, inner):
            weights_of = jnp.exp(scores[number] - top)
            totals[...] += jnp.sum(weights_of.reshape(BLOCK // 8, 8, lanes), axis=0)
            attended[...] += dot(values_turned[span(group, HD), span(number, BLOCK)], weights_of.astype(low))
            return inner

        lax.fori_loop(0, diagonal + 1, weigh, 0)
        total = jnp.sum(totals[...], axis=0, keepdims=True)
        log_totals[index] = top + jnp.log(total)
        done = attended[...] / total
        high = done.astype(low)
        rest = (done - high.astype(f32)).astype(low)
        for place in range(ratio):
            at = slice(place * BLOCK, (place + 1) * BLOCK)
            attended_turned[span(group * ratio + place, HD), span(block, BLOCK)] = high[:, at]
            attended_rest[span(group * ratio + place, HD), span(block, BLOCK)] = rest[:, at]
        return carry

    lax.fori_loop(0, KVH * blocks, attend, 0)

    pushes[4].wait_recv()
    local[3].wait()

    def close(number, carry):
        at = span(number, BLOCK)
        branch = dot(attended_turned[:, at].T, out_mat[...])
        total = tokens[at].astype(f32) + branch
        middle[at] = total
        inverse = lax.rsqrt(jnp.mean(total * total, axis=-1, keepdims=True) + norm_eps)
        hidden_two[at] = (total * inverse * vectors_full[4:5]).astype(low)
        return carry

    lax.fori_loop(0, blocks, close, 0)

    stores = [
        pltpu.make_async_copy(source, goal, store.at[number])
        for number, (source, goal) in enumerate(
            ((query_mat, query_full), (key_mat, key_full), (value_mat, value_full), (out_mat, out_full))
        )
    ]
    for copy in stores:
        copy.start()
    for copy in pushes[:5]:
        copy.wait_send()
    for copy in pushes[5:]:
        copy.wait()

    @pl.when(rank == 0)
    def _():
        pair_push.wait_send()

    for copy in stores:
        copy.wait()


def front(tokens, lines, angles, query_w, key_w, value_w, out_w, gate_w, up_w, down_w, spread):
    rows, width = tokens.shape
    low, f32 = jnp.bfloat16, jnp.float32
    blocks = rows // BLOCK
    kv_width = KVH * HD
    lanes = H // KVH * BLOCK
    anywhere = pl.BlockSpec(memory_space=pl.ANY)
    vmem = pl.BlockSpec(memory_space=pltpu.VMEM)
    shape = jax.ShapeDtypeStruct
    outs = [
        (shape((rows, width), low), vmem),
        (shape((rows, width), f32), vmem),
        (shape((width, rows), low), vmem),
        (shape((KVH * blocks, HD, lanes), low), vmem),
        (shape((KVH, rows * spread, HD), low), vmem),
        (shape((KVH, rows * spread, HD), low), vmem),
        (shape((kv_width, rows * spread), low), vmem),
        (shape((H * HD, rows), low), vmem),
        (shape((H * HD, rows), low), vmem),
        (shape((KVH * blocks, 1, lanes), f32), vmem),
        (shape((8, width), f32), vmem),
        (shape((width, H * HD), low), anywhere),
        (shape((width, kv_width), low), anywhere),
        (shape((width, kv_width), low), anywhere),
        (shape((H * HD, width), low), anywhere),
        (shape(gate_w.shape, low), anywhere),
        (shape(up_w.shape, low), anywhere),
        (shape(down_w.shape, low), anywhere),
    ]
    return pl.pallas_call(
        front_kernel,
        out_shape=tuple(item for item, _ in outs),
        in_specs=[vmem] * 6 + [anywhere] * 8,
        out_specs=tuple(spec for _, spec in outs),
        scratch_shapes=[
            pltpu.VMEM((width, H * HD), low),
            pltpu.VMEM((width, kv_width), low),
            pltpu.VMEM((width, kv_width), low),
            pltpu.VMEM((H * HD, width), low),
            pltpu.VMEM((8, width // spread), f32),
            pltpu.VMEM((8, width // spread), f32),
            pltpu.VMEM((2, HD // 2, rows), f32),
            pltpu.VMEM((rows, width), low),
            pltpu.VMEM((rows, width), f32),
            pltpu.VMEM((kv_width, rows * spread), low),
            pltpu.VMEM((2, rows, kv_width), low),
            pltpu.VMEM((2, rows, kv_width), low),
            pltpu.VMEM((blocks * spread, BLOCK, lanes), f32),
            pltpu.VMEM((8, lanes), f32),
            pltpu.VMEM((8, lanes), f32),
            pltpu.VMEM((HD, lanes), f32),
            pltpu.SemaphoreType.DMA((5,)),
            pltpu.SemaphoreType.DMA((9,)),
            pltpu.SemaphoreType.DMA((9,)),
            pltpu.SemaphoreType.DMA((4,)),
        ],
        compiler_params=pltpu.CompilerParams(
            collective_id=1, has_side_effects=True, vmem_limit_bytes=60 * 1024 * 1024
        ),
    )(tokens, *lines, angles, query_w, key_w, value_w, out_w, gate_w, up_w, down_w)


def back_kernel(
    chunks,
    length,
    hidden_two,
    upstream,
    vectors,
    tokens_hbm,
    middle_hbm,
    turned_hbm,
    queries_hbm,
    keys_hbm,
    values_hbm,
    keys_turned_hbm,
    attended_hbm,
    rest_hbm,
    log_hbm,
    query_hbm,
    key_hbm,
    value_hbm,
    out_hbm,
    gate_hbm,
    gate_other,
    up_hbm,
    up_other,
    down_hbm,
    down_other,
    angle_hbm,
    block_out,
    input_out,
    gate_out,
    up_out,
    down_out,
    query_out,
    key_out,
    value_out,
    out_out,
    small_out,
    acc,
    split,
    inward,
    mids,
    last,
    away,
    landed,
    gate_buf,
    up_buf,
    down_buf,
    final,
    back,
    spare,
    turned,
    gate_back,
    up_back,
    product,
    product_turned,
    branch,
    heads_turned,
    queries,
    heads_grad,
    keys,
    values,
    keys_turned,
    log_totals,
    delta,
    hidden_turned,
    tokens,
    square,
    key_mat,
    value_mat,
    angles,
    probs,
    score_grad,
    query_sum,
    pair_sum,
    pair_far,
    pair_low,
    gain_sum,
    send,
    recv,
    freed,
    gsend,
    grecv,
    load,
    store,
    plain,
    psend,
    precv,
):
    rank = lax.axis_index("group")
    partner = 1 - rank
    rows, width = hidden_two.shape
    share = width // 2
    columns = gate_hbm.shape[1]
    half_hidden = columns // 2
    tiles = half_hidden // LANES
    blocks = rows // BLOCK
    ratio = H // KVH
    low, f32 = jnp.bfloat16, jnp.float32
    tall = LANES // 2
    wide_blocks = width // LANES

    def seat(number):
        lot, place = divmod(number, 3)
        return tiles + lot // 2, lot % 2, place * share

    small_chunk, small_lot, small_row = seat(2 * wide_blocks + 2)

    def tile_writes(chunk):
        found = []
        for lot in (0, 1):
            at = pl.multiple_of(chunk * LANES + lot * half_hidden, LANES)
            for number, goal in enumerate((gate_out, up_out)):
                found.append(
                    pltpu.make_async_copy(
                        acc.at[chunk, lot, pl.ds(number * share, share)],
                        goal.at[:, pl.ds(at, LANES)],
                        store.at[chunk, lot, number],
                    )
                )
            for block in range(wide_blocks):
                found.append(
                    pltpu.make_async_copy(
                        acc.at[chunk, lot, pl.ds(2 * share + block * tall, tall)],
                        down_out.at[
                            pl.ds(pl.multiple_of(chunk * LANES + lot * tall, tall), tall),
                            pl.ds(block * LANES, LANES),
                        ],
                        store.at[chunk, lot, 2 + block],
                    )
                )
        return found

    def rest_writes(chunk):
        goals = [(out_out, block) for block in range(wide_blocks)]
        goals += [(key_out, 0), (value_out, 0)]
        goals += [(query_out, block) for block in range(wide_blocks)]
        found = []
        for number, (goal, block) in enumerate(goals):
            where, lot, row = seat(number)
            if where == chunk:
                found.append(
                    pltpu.make_async_copy(
                        acc.at[where, lot, pl.ds(row, share)],
                        goal.at[:, pl.ds(block * LANES, LANES)],
                        store.at[where, lot, row // share],
                    )
                )
        if chunk == small_chunk:
            for block in range(wide_blocks):
                found.append(
                    pltpu.make_async_copy(
                        acc.at[chunk, small_lot, pl.ds(small_row + block * 16, 16)],
                        small_out.at[:, pl.ds(block * LANES, LANES)],
                        store.at[chunk, small_lot, 2 + block],
                    )
                )
        return found

    def start_writes(chunk):
        @pl.when(chunk < tiles)
        def _():
            for copy in tile_writes(chunk):
                copy.start()

        for rest in range(tiles, chunks):

            @pl.when(chunk == rest)
            def _():
                for copy in rest_writes(rest):
                    copy.start()

    ladder = Ladder(chunks, length, acc, split, inward, mids, last, send, recv, freed, start_writes)
    enter(ladder, partner)
    tick = ladder.tick

    early = [
        pltpu.make_async_copy(source, goal, plain.at[number])
        for number, (source, goal) in enumerate(
            (
                (middle_hbm, spare),
                (queries_hbm, queries),
                (keys_hbm, keys),
                (values_hbm, values),
                (keys_turned_hbm, keys_turned),
                (attended_hbm, heads_turned),
                (log_hbm, log_totals),
                (rest_hbm, hidden_turned),
                (out_hbm, square),
                (key_hbm, key_mat),
                (value_hbm, value_mat),
                (angle_hbm.at[:, :, span(rank, rows)], angles),
            )
        )
    ]

    def loads(tile):
        slot = lax.rem(tile, 2)
        found = []
        for lot in (0, 1):
            at = pl.ds(pl.multiple_of(tile * LANES + lot * half_hidden, LANES), LANES)
            goal_columns = pl.ds(lot * LANES, LANES)
            for side, gate_side, up_side in ((rank, gate_hbm, up_hbm), (partner, gate_other, up_other)):
                number = len(found)
                goal_rows = pl.ds(pl.multiple_of(side * share, 16), share)
                found.append(
                    pltpu.make_async_copy(
                        gate_side.at[:, at], gate_buf.at[slot, goal_rows, goal_columns], load.at[slot, number]
                    )
                )
                found.append(
                    pltpu.make_async_copy(
                        up_side.at[:, at], up_buf.at[slot, goal_rows, goal_columns], load.at[slot, number + 1]
                    )
                )
        at = pl.ds(pl.multiple_of(tile * LANES, LANES), LANES)
        for side, source in ((rank, down_hbm), (partner, down_other)):
            found.append(
                pltpu.make_async_copy(source.at[at], down_buf.at[slot, span(side, LANES)], load.at[slot, len(found)])
            )
        return found

    def across(chunk):
        slot = lax.rem(chunk, 2)
        return pltpu.make_async_remote_copy(
            src_ref=away.at[slot],
            dst_ref=landed.at[slot],
            send_sem=gsend.at[slot],
            recv_sem=grecv.at[slot],
            device_id={"group": partner},
            device_id_type=MESH,
        )

    def finish(chunk):
        across(chunk).wait()
        slot = lax.rem(chunk, 2)
        for lot in (0, 1):
            mine = acc[chunk, lot].astype(f32)
            acc[chunk, lot] = (mine + landed[slot, lot].astype(f32)).astype(low)

    for copy in loads(0):
        copy.start()
    for copy in early:
        copy.start()
    final[...] = jnp.zeros_like(final)
    back[...] = jnp.zeros_like(back)
    for block in range(blocks):
        at = slice(block * BLOCK, (block + 1) * BLOCK)
        turned[:, at] = hidden_two[at].T

    def put(target, where, value, first_row):
        for lot in (0, 1):
            target[where, lot, pl.ds(first_row, share)] = value[:, lot * LANES : (lot + 1) * LANES].astype(low)

    def put_down(target, where, value):
        for lot in (0, 1):
            for block in range(wide_blocks):
                target[where, lot, pl.ds(2 * share + block * tall, tall)] = value[
                    lot * tall : (lot + 1) * tall, block * LANES : (block + 1) * LANES
                ].astype(low)

    def compute(tile):
        slot = lax.rem(tile, 2)

        for number in range(blocks):
            at = slice(number * BLOCK, (number + 1) * BLOCK)
            hidden = hidden_two[at]
            gate_pre = dot(hidden, gate_buf[slot])
            up_pre = dot(hidden, up_buf[slot])
            grad = dot_nt(upstream[at], down_buf[slot])
            sigmoid = 1.0 / (1.0 + jnp.exp(-gate_pre))
            swish = gate_pre * sigmoid
            unit = (swish * up_pre).astype(low)
            gate_grad = (grad * up_pre * sigmoid * (1.0 + gate_pre * (1.0 - sigmoid))).astype(low)
            up_grad = (grad * swish).astype(low)
            product[at] = unit
            gate_back[at] = gate_grad
            up_back[at] = up_grad
            product_turned[:, at] = unit.T
            final[at] += dot(unit, down_buf[slot])
            back[at] += dot_nt(gate_grad, gate_buf[slot]) + dot_nt(up_grad, up_buf[slot])
        for owner, target, where in ((partner, away, slot), (rank, acc, tile)):
            some = turned[pl.ds(pl.multiple_of(owner * share, 16), share)]
            put(target, where, dot(some, gate_back[...]), 0)
            put(target, where, dot(some, up_back[...]), share)
            some = product_turned[span(owner, LANES)]
            put_down(target, where, dot(some, upstream[...]))

    pace = 2

    def tile_step(tile, carry):
        for copy in loads(tile):
            copy.wait()

        @pl.when(tile + 1 < tiles)
        def _():
            for copy in loads(tile + 1):
                copy.start()

        compute(tile)

        @pl.when(tile >= 1)
        def _():
            finish(tile - 1)

        across(tile).start()

        @pl.when(lax.rem(tile, pace) == pace - 1)
        def _():
            tick(lax.div(tile, pace))

        return carry

    lax.fori_loop(0, tiles, tile_step, 0)
    clock = tiles // pace

    finish(tiles - 1)
    tick(clock)
    clock += 1
    for copy in early:
        copy.wait()
    gain_sum[...] = jnp.zeros_like(gain_sum)

    def norm_two(number, carry):
        at = span(number, BLOCK)
        total = spare[at]
        tokens[at] = (total + final[at]).astype(low)
        inverse = lax.rsqrt(jnp.mean(total * total, axis=-1, keepdims=True) + norm_eps)
        normed = total * inverse
        grad = back[at]
        gain_sum[0:1] += jnp.sum(grad * normed, axis=0, keepdims=True)
        scaled = grad * vectors[4:5]
        grad = upstream[at].astype(f32) + inverse * (
            scaled - normed * jnp.mean(scaled * normed, axis=-1, keepdims=True)
        )
        back[at] = grad
        branch[at] = grad.astype(low)
        return carry

    lax.fori_loop(0, blocks, norm_two, 0)
    block_write = pltpu.make_async_copy(tokens, block_out, plain.at[0])
    block_write.start()
    tick(clock)
    clock += 1

    def scatter(first, values_of, target, owner_is_me):
        for block in range(values_of.shape[1] // LANES):
            where, lot, row = seat(first + block)
            slot = where if owner_is_me else where % 2
            target[slot, lot, pl.ds(row, share)] = values_of[:, block * LANES : (block + 1) * LANES].astype(low)

    both_sides = ((partner, away, False), (rank, acc, True))

    for owner, target, mine in both_sides:
        some = heads_turned[pl.ds(pl.multiple_of(owner * share, 16), share)]
        lot_columns = (wide_blocks - 1) * LANES
        scatter(0, dot(some, branch[:, :lot_columns]), target, mine)
    across(tiles).start()
    finished_grad = dot_nt(square[...], branch[...]).astype(low)
    for head in range(H):
        group, place = divmod(head, ratio)
        lanes = slice(place * BLOCK, (place + 1) * BLOCK)
        some = finished_grad[head * HD : (head + 1) * HD]
        features = slice(head * HD, (head + 1) * HD)
        result = heads_turned[features].astype(f32) + hidden_turned[features].astype(f32)
        overlap = jnp.sum(some.astype(f32) * result, axis=0, keepdims=True)
        for block in range(blocks):
            at = slice(block * BLOCK, (block + 1) * BLOCK)
            heads_grad[group * blocks + block, :, lanes] = some[:, at]
            delta[group * blocks + block, :, lanes] = overlap[:, at]
    last_out = LANES * (wide_blocks - 1)
    next_mat = pltpu.make_async_copy(query_hbm, square, plain.at[1])
    next_mat.start()
    next_turned = pltpu.make_async_copy(turned_hbm, hidden_turned, plain.at[2])
    next_turned.start()
    tick(clock)
    clock += 1
    block_write.wait()
    tokens_load = pltpu.make_async_copy(tokens_hbm, tokens, plain.at[0])
    tokens_load.start()
    finish(tiles)
    pair_sum[...] = jnp.zeros_like(pair_sum)

    key_place = lax.broadcasted_iota(jnp.int32, (BLOCK, BLOCK), 0)
    query_place = lax.broadcasted_iota(jnp.int32, (BLOCK, BLOCK), 1)
    starts = [0]
    for block in range(blocks):
        starts.append(starts[-1] + blocks + block + 1)
    per_group = starts[-1]

    wide_keys = jnp.concatenate([key_place] * ratio, axis=1)
    wide_queries = jnp.concatenate([query_place] * ratio, axis=1)

    def attend(group, block, number, masked):
        index = group * blocks + block
        at = span(number, BLOCK)
        scores = dot(keys[group, at], queries[index])
        if masked:
            scores = jnp.where(wide_keys <= wide_queries, scores, masked_score)
        weights = jnp.exp(scores - log_totals[index])
        weights_grad = dot(values[group, at], heads_grad[index])
        probs[...] = weights.astype(low)
        score_grad[...] = (weights * (weights_grad - delta[index])).astype(low)
        rows_of = span(group, HD)
        pair_sum[1, rows_of, at] += dot_nt(heads_grad[index], probs[...])
        pair_sum[0, rows_of, at] += dot_nt(queries[index], score_grad[...])
        query_sum[...] += dot(keys_turned[rows_of, at], score_grad[...])

    beat = 4

    def attend_step(step, carry):
        group, inside = lax.div(step, per_group), lax.rem(step, per_group)
        block, first = jnp.int32(0), jnp.int32(0)
        for number in range(1, blocks):
            reached = inside >= starts[number]
            block = jnp.where(reached, number, block)
            first = jnp.where(reached, starts[number], first)
        number = inside - first
        diagonal = rank * blocks + block

        @pl.when(number == 0)
        def _():
            query_sum[...] = jnp.zeros_like(query_sum)

        @pl.when(number < diagonal)
        def _():
            attend(group, block, number, False)

        @pl.when(number == diagonal)
        def _():
            attend(group, block, number, True)

        @pl.when(number == blocks + block)
        def _():
            at = span(block, BLOCK)
            cosine, sine = angles[0, :, at], angles[1, :, at]
            for place in range(ratio):
                lanes = slice(place * BLOCK, (place + 1) * BLOCK)
                head = turn_back(query_sum[:, lanes] * (1.0 / math.sqrt(HD)), cosine, sine)
                turned[span(group * ratio + place, HD), at] = head.astype(low)

        @pl.when(lax.rem(step, beat) == beat - 1)
        def _():
            tick(clock + lax.div(step, beat))

        return carry

    steps = KVH * per_group
    lax.fori_loop(0, steps, attend_step, 0)
    clock += steps // beat

    pair_push = pltpu.make_async_remote_copy(
        src_ref=pair_sum.at[:, :, pl.ds(0, rows)],
        dst_ref=pair_far,
        send_sem=psend,
        recv_sem=precv,
        device_id={"group": partner},
        device_id_type=MESH,
    )

    @pl.when(rank == 1)
    def _():
        pair_push.start()

    next_mat.wait()
    next_turned.wait()
    tokens_load.wait()
    tick(clock)
    clock += 1
    for owner, target, mine in both_sides:
        some = hidden_turned[pl.ds(pl.multiple_of(owner * share, 16), share)]
        scatter(wide_blocks + 2, dot_nt(some, turned[...]), target, mine)
        some = heads_turned[pl.ds(pl.multiple_of(owner * share, 16), share)]
        scatter(wide_blocks - 1, dot(some, branch[:, last_out:]), target, mine)

    @pl.when(rank == 0)
    def _():
        pair_push.wait_recv()
        pair_sum[:, :, :rows] += pair_far[...]

    own = span(rank, rows)
    for head in range(KVH):
        at = slice(head * HD, (head + 1) * HD)
        pair_low[0, at] = turn_back(pair_sum[0, at, own], angles[0], angles[1]).astype(low)
    pair_low[1] = pair_sum[1, :, own].astype(low)
    for owner, target, mine in both_sides:
        some = hidden_turned[pl.ds(pl.multiple_of(owner * share, 16), share)]
        scatter(wide_blocks, dot_nt(some, pair_low[0]), target, mine)
        scatter(wide_blocks + 1, dot_nt(some, pair_low[1]), target, mine)
    across(tiles + 1).start()
    tick(clock)
    clock += 1

    def norm_one(number, carry):
        at = span(number, BLOCK)
        grad = dot_nt(turned[:, at].T, square[...])
        grad += dot_nt(pair_low[0, :, at].T, key_mat[...]) + dot_nt(pair_low[1, :, at].T, value_mat[...])
        residual = tokens[at].astype(f32)
        inverse = lax.rsqrt(jnp.mean(residual * residual, axis=-1, keepdims=True) + norm_eps)
        normed = residual * inverse
        gain_sum[1:2] += jnp.sum(grad * normed, axis=0, keepdims=True)
        scaled = grad * vectors[0:1]
        back[at] += inverse * (scaled - normed * jnp.mean(scaled * normed, axis=-1, keepdims=True))
        return carry

    lax.fori_loop(0, blocks, norm_one, 0)
    input_write = pltpu.make_async_copy(back, input_out, plain.at[2])
    input_write.start()

    ones = jnp.ones((16, rows), low)
    query_bias = dot_nt(ones, turned[...])
    pair_bias = jnp.concatenate(
        [
            dot_nt(ones, pair_low[0]),
            dot_nt(ones, pair_low[1]),
            jnp.zeros((16, width - 2 * KVH * HD), f32),
        ],
        axis=1,
    )
    line = lax.broadcasted_iota(jnp.int32, (16, width), 0)
    small = jnp.where(line == 0, gain_sum[1:2], 0.0)
    small = jnp.where(line == 1, query_bias, small)
    small = jnp.where(line == 2, pair_bias, small)
    small = jnp.where(line == 3, gain_sum[0:1], small).astype(low)
    finish(tiles + 1)
    left = small_row + 16 * wide_blocks
    for target, slot in ((away, small_chunk % 2), (acc, small_chunk)):
        for block in range(wide_blocks):
            target[slot, small_lot, pl.ds(small_row + 16 * block, 16)] = small[:, block * LANES : (block + 1) * LANES]
        target[slot, small_lot, pl.ds(left, ROWS - left)] = jnp.zeros((ROWS - left, LANES), low)
    across(tiles + 2).start()
    tick(clock)
    clock += 1
    finish(tiles + 2)

    def remaining(time, carry):
        tick(time)
        return carry

    lax.fori_loop(clock, chunks + last_offset(length), remaining, 0)
    input_write.wait()

    @pl.when(rank == 1)
    def _():
        pair_push.wait_send()

    def drain(chunk, carry):
        for copy in tile_writes(chunk):
            copy.wait()
        return carry

    lax.fori_loop(0, tiles, drain, 0)
    for chunk in range(tiles, chunks):
        for copy in rest_writes(chunk):
            copy.wait()


def backward(front_parts, upstream, tokens, angles, gate_w, up_w, down_w, replicas, spread):
    (
        hidden_two,
        middle,
        turned_one,
        queries,
        keys,
        values,
        keys_turned,
        attended_turned,
        attended_rest,
        log_totals,
        vectors,
        query_full,
        key_full,
        value_full,
        out_full,
        gate_other,
        up_other,
        down_other,
    ) = front_parts
    rows, width = hidden_two.shape
    columns = gate_w.shape[1]
    tiles = columns // (2 * LANES)
    chunks = tiles + 3
    length = replicas // 4
    slots = Ladder.slots_of(length)
    low, f32 = jnp.bfloat16, jnp.float32
    pair = 2 * LANES
    kv_width = KVH * HD
    anywhere = pl.BlockSpec(memory_space=pl.ANY)
    vmem = pl.BlockSpec(memory_space=pltpu.VMEM)
    shape = jax.ShapeDtypeStruct
    inputs = (
        hidden_two,
        upstream,
        vectors,
        tokens,
        middle,
        turned_one,
        queries,
        keys,
        values,
        keys_turned,
        attended_turned,
        attended_rest,
        log_totals,
        query_full,
        key_full,
        value_full,
        out_full,
        gate_w,
        gate_other,
        up_w,
        up_other,
        down_w,
        down_other,
        angles,
    )
    return pl.pallas_call(
        functools.partial(back_kernel, chunks, length),
        out_shape=(
            shape((rows, width), low),
            shape((rows, width), f32),
            shape((width // 2, columns), low),
            shape((width // 2, columns), low),
            shape((columns // 2, width), low),
            shape((width // 2, H * HD), low),
            shape((width // 2, kv_width), low),
            shape((width // 2, kv_width), low),
            shape((H * HD // 2, width), low),
            shape((16, width), low),
        ),
        in_specs=[vmem] * 3 + [anywhere] * (len(inputs) - 3),
        out_specs=(anywhere,) * 10,
        scratch_shapes=[
            pltpu.VMEM((chunks, 2, ROWS, LANES), low),
            pltpu.VMEM((4, 2, HALF, LANES), low),
            pltpu.VMEM((slots, 2, HALF, LANES), low),
            pltpu.VMEM((4, 2, QUARTER, LANES), low),
            pltpu.VMEM((4, 2, QUARTER, LANES), low),
            pltpu.VMEM((2, 2, ROWS, LANES), low),
            pltpu.VMEM((2, 2, ROWS, LANES), low),
            pltpu.VMEM((2, width, pair), low),
            pltpu.VMEM((2, width, pair), low),
            pltpu.VMEM((2, pair, width), low),
            pltpu.VMEM((rows, width), f32),
            pltpu.VMEM((rows, width), f32),
            pltpu.VMEM((rows, width), f32),
            pltpu.VMEM((width, rows), low),
            pltpu.VMEM((rows, pair), low),
            pltpu.VMEM((rows, pair), low),
            pltpu.VMEM((rows, pair), low),
            pltpu.VMEM((pair, rows), low),
            pltpu.VMEM((rows, width), low),
            pltpu.VMEM((H * HD, rows), low),
            pltpu.VMEM(queries.shape, low),
            pltpu.VMEM(queries.shape, low),
            pltpu.VMEM(keys.shape, low),
            pltpu.VMEM(values.shape, low),
            pltpu.VMEM(keys_turned.shape, low),
            pltpu.VMEM(log_totals.shape, f32),
            pltpu.VMEM(log_totals.shape, f32),
            pltpu.VMEM((width, rows), low),
            pltpu.VMEM((rows, width), low),
            pltpu.VMEM((width, width), low),
            pltpu.VMEM((width, kv_width), low),
            pltpu.VMEM((width, kv_width), low),
            pltpu.VMEM((2, HD // 2, rows), f32),
            pltpu.VMEM((BLOCK, queries.shape[2]), low),
            pltpu.VMEM((BLOCK, queries.shape[2]), low),
            pltpu.VMEM(queries.shape[1:], f32),
            pltpu.VMEM((2, kv_width, rows * spread), f32),
            pltpu.VMEM((2, kv_width, rows), f32),
            pltpu.VMEM((2, kv_width, rows), low),
            pltpu.VMEM((8, width), f32),
            pltpu.SemaphoreType.DMA((7, slots, 2)),
            pltpu.SemaphoreType.DMA((7, slots, 2)),
            pltpu.SemaphoreType.REGULAR((3, 2)),
            pltpu.SemaphoreType.DMA((2,)),
            pltpu.SemaphoreType.DMA((2,)),
            pltpu.SemaphoreType.DMA((2, 10)),
            pltpu.SemaphoreType.DMA((chunks, 2, 2 + width // LANES)),
            pltpu.SemaphoreType.DMA((12,)),
            pltpu.SemaphoreType.DMA,
            pltpu.SemaphoreType.DMA,
        ],
        compiler_params=pltpu.CompilerParams(
            collective_id=2, has_side_effects=True, vmem_limit_bytes=63 * 1024 * 1024
        ),
    )(*inputs)


SLAB = 64


def last_kernel(count, *refs):
    sources, small, block_low, input_low = refs[:count], refs[count], refs[count + 1], refs[count + 2]
    outs = refs[count + 3 :]
    goals, lines, block_out, input_out = outs[:count], outs[count : count + 5], outs[count + 5], outs[count + 6]
    rest = outs[count + 7 :]
    narrow, wide = rest[:count], rest[count : 2 * count]
    load, store, plain = rest[2 * count :]
    rank = lax.axis_index("group")
    passed = [
        pltpu.make_async_copy(block_low, block_out, plain.at[0]),
        pltpu.make_async_copy(input_low, input_out, plain.at[1]),
    ]
    jobs = []
    for number, source in enumerate(sources):
        rows, columns = source.shape
        size = SLAB * max(1, 4864 // columns)
        for first in range(0, rows, size):
            at = pl.ds(first, min(size, rows - first))
            place = len(jobs)
            jobs.append(
                (
                    number,
                    first,
                    min(size, rows - first),
                    pltpu.make_async_copy(source.at[at], narrow[number].at[at], load.at[place]),
                    pltpu.make_async_copy(wide[number].at[at], goals[number].at[at], store.at[place]),
                )
            )
    for job in jobs:
        job[3].start()
    for copy in passed:
        copy.start()
    for line, (row, first, goal) in enumerate(
        ((0, 0, lines[0]), (1, 0, lines[1]), (2, 0, lines[2]), (2, KVH * HD, lines[3]), (3, 0, lines[4]))
    ):
        size = goal.shape[0]
        both = small[...][row : row + 1].astype(jnp.float32)
        mine = jnp.where(rank == 0, both[:, first : first + size], both[:, first + size : first + 2 * size])
        goal[...] = mine.reshape(size)
    for number, first, size, read, write in jobs:
        read.wait()

        def cast(step, carry):
            at = pl.ds(pl.multiple_of(first + step * 32, 32), 32)
            wide[number][at] = narrow[number][at].astype(jnp.float32)
            return carry

        lax.fori_loop(0, size // 32, cast, 0)
        write.start()
    for job in jobs:
        job[4].wait()
    for copy in passed:
        copy.wait()


def finish_outputs(sums, small, block_low, input_low, sizes):
    low, f32 = jnp.bfloat16, jnp.float32
    anywhere = pl.BlockSpec(memory_space=pl.ANY)
    vmem = pl.BlockSpec(memory_space=pltpu.VMEM)
    shape = jax.ShapeDtypeStruct
    count = len(sums)
    jobs = 0
    for item in sums:
        rows, columns = item.shape
        jobs += -(-rows // (SLAB * max(1, 4864 // columns)))
    return pl.pallas_call(
        functools.partial(last_kernel, count),
        out_shape=tuple(
            [shape(item.shape, f32) for item in sums]
            + [shape((size,), f32) for size in sizes]
            + [shape(block_low.shape, block_low.dtype), shape(input_low.shape, input_low.dtype)]
        ),
        in_specs=[anywhere] * count + [vmem] + [anywhere] * 2,
        out_specs=tuple([anywhere] * count + [vmem] * 5 + [anywhere] * 2),
        scratch_shapes=[pltpu.VMEM(item.shape, low) for item in sums]
        + [pltpu.VMEM(item.shape, f32) for item in sums]
        + [pltpu.SemaphoreType.DMA((jobs,)), pltpu.SemaphoreType.DMA((jobs,)), pltpu.SemaphoreType.DMA((2,))],
        compiler_params=pltpu.CompilerParams(vmem_limit_bytes=56 * 1024 * 1024),
    )(*sums, small, block_low, input_low)


def local(
    tokens,
    cotangent,
    first_gain,
    query_weight,
    query_bias,
    key_weight,
    key_bias,
    value_weight,
    value_bias,
    output_weight,
    second_gain,
    gate_weight,
    up_weight,
    down_weight,
):
    spread = lax.axis_size("group")
    rows = tokens.shape[0]
    lines = (first_gain, query_bias, key_bias, value_bias, second_gain)
    angles = jnp.asarray(tables(rows * spread, HD))
    parts = front(
        tokens,
        lines,
        angles,
        query_weight,
        key_weight,
        value_weight,
        output_weight,
        gate_weight,
        up_weight,
        down_weight,
        spread,
    )
    (
        block_output,
        input_grad,
        gate_sum,
        up_sum,
        down_sum,
        query_sum,
        key_sum,
        value_sum,
        out_sum,
        small,
    ) = backward(
        parts, cotangent, tokens, angles, gate_weight, up_weight, down_weight, lax.axis_size("replica"), spread
    )

    sizes = [item.shape[0] for item in lines]
    (
        gate_grad,
        up_grad,
        down_grad,
        query_grad,
        out_grad,
        key_grad,
        value_grad,
        first_gain_grad,
        query_bias_grad,
        key_bias_grad,
        value_bias_grad,
        second_gain_grad,
        block_output,
        input_grad,
    ) = finish_outputs(
        (gate_sum, up_sum, down_sum, query_sum, out_sum, key_sum, value_sum), small, block_output, input_grad, sizes
    )
    return (
        block_output,
        input_grad,
        first_gain_grad,
        query_grad,
        query_bias_grad,
        key_grad,
        key_bias_grad,
        value_grad,
        value_bias_grad,
        out_grad,
        second_gain_grad,
        gate_grad,
        up_grad,
        down_grad,
    )


def solution(mesh):
    return jax.shard_map(
        local,
        mesh=mesh,
        in_specs=(
            P(("replica", "group"), None),
            P(("replica", "group"), None),
            P("group"),
            P("group", None),
            P("group"),
            P("group", None),
            P("group"),
            P("group", None),
            P("group"),
            P("group", None),
            P("group"),
            P("group", None),
            P("group", None),
            P("group", None),
        ),
        out_specs=(
            P(("replica", "group"), None),
            P(("replica", "group"), None),
            P("group"),
            P("group", None),
            P("group"),
            P("group", None),
            P("group"),
            P("group", None),
            P("group"),
            P("group", None),
            P("group"),
            P("group", None),
            P("group", None),
            P("group", None),
        ),
        check_vma=False,
    )
```

time: 1360 us -> 448 us (0.33)
  waiting for transfers between devices: 781 us -> 0 us
  Pallas kernels: 0 us -> 447 us
  matrix products: 344 us -> 0 us
  other arithmetic: 97.6 us -> 0 us
  blocking collectives: 60.3 us -> 0 us
  local copies, waits for them, and re-layouts: 53.3 us -> 0 us
  between operations: 17.8 us -> 0.84 us
    psum x1 -> x0, waiting for transfers between devices: 710 us -> none  [local(): lax.psum((all_parts[0], all_parts[1], all_parts[2], all_parts[3], all_par...]
    pallas_call x0 -> x3, Pallas kernels: none -> 447 us  [the longest x1 289 us: backward(): pl.pallas_call(functools.partial(back_kernel, chunks, length), out_shape=...]
    dot_general x33 -> x0, matrix products: 344 us -> none  [the longest x2 50.4 us: local(): jnp.einsum('tgd,sd->gts', head_grad, value_all[:, head], preferred_elemen...]
    reduce_scatter x9 -> x0, waiting for transfers between devices: 67.7 us -> none  [the longest x1 30.4 us: local(): lax.psum_scatter(up_wgrad, 'group', scatter_dimension=0, tiled=True)]
    convert_element_type x13 -> x0, other arithmetic: 57.2 us -> none  [the longest x2 55.6 us: local(): score_grad = (probs * (prob_grad - jnp.sum(probs * prob_grad, axis=-1, ke...]
    unnamed x151 -> x0, local copies, waits for them, and re-layouts: 50 us -> none
    psum x1 -> x0, blocking collectives: 45.7 us -> none  [local(): lax.psum((all_parts[0], all_parts[1], all_parts[2], all_parts[3], all_par...]
    reduce_sum x6 -> x0, other arithmetic: 22.3 us -> none  [the longest x2 19.6 us: local(): jnp.sum(jnp.exp(scores - top), axis=-1, keepdims=True)]
  transfers between devices with their start and end apart: 15 -> 0, of which waited for: 4 -> 0; matrix products, arithmetic and copies ran while one was open for 18% -> 0% of each run, Pallas kernels for 0% -> 0%
where the time goes in v1:
time: 448 us
  Pallas kernels  447 us (100%)
    pallas_call x1, Pallas kernels, backward(): pl.pallas_call(functools.partial(back_kernel, chunks, length), out_shape=...  289 us
    pallas_call x1, Pallas kernels, finish_outputs(): pl.pallas_call(functools.partial(last_kernel, count), out_shape=tuple([sh...  128 us
    pallas_call x1, Pallas kernels, front(): pl.pallas_call(front_kernel, out_shape=tuple((item for item, _ in outs)),...  29.4 us

profile of v1, /device:TPU:0, one launch (start us, length us, event | category | flops | bytes accessed | tf_op | source)
XLA Modules:
  0.0 447.6 jit_solution(13554353685292746673)
XLA Ops:
  0.6 29.4 %shard_map.254 = (bf16[768,896]{1,0:T(8,128)(2,1)}, f32[768,896]{1,0:T(8,128)}, bf16[896,768]{1,0:T(8,128)(2,1)}, bf16[6,64,1792]{2,1,0:T(8,128)(2,1)}, bf16[2,1...) custom-call(bf16[768,896]{1,0:T(8,128)(2,1)} %tokens_hbm.1, ...), custom_call_target="tpu_custom_call" | custom-call | tf_op jit(solution)/shard_map/pallas_call | solution.py:542
  30.0 289.3 %shard_map.255 = (bf16[768,896]{1,0:T(8,128)(2,1)}, f32[768,896]{1,0:T(8,128)}, bf16[448,4864]{1,0:T(8,128)(2,1)}, bf16[448,4864]{1,0:T(8,128)(2,1)}, bf16[2432,...) custom-call(bf16[768,896]{1,0:T(8,128)(2,1)} %get-tuple-element.56.h, ...), custom_call_target="tpu_custom_call" | custom-call | tf_op jit(solution)/shard_map/pallas_call | solution.py:1190
  319.3 128.1 %shard_map.256 = (f32[448,4864]{1,0:T(8,128)}, f32[448,4864]{1,0:T(8,128)}, f32[2432,896]{1,0:T(8,128)}, f32[448,896]{1,0:T(8,128)}, f32[448,896]{1,0:T(8,128)},...) custom-call(bf16[448,4864]{1,0:T(8,128)(2,1)} %get-tuple-element.74., ...), custom_call_target="tpu_custom_call" | custom-call | tf_op jit(solution)/shard_map/pallas_call | solution.py:1332

commit v2 on v1

--- a/solution.py
+++ b/solution.py
@@ -22,8 +22,7 @@
 MESH = pl.DeviceIdType.MESH
 LANES = 128
 ROWS = 1344
-HALF = ROWS // 2
-QUARTER = ROWS // 4
+SHORT = 896
 
 
 class Ladder:
@@ -32,8 +31,9 @@
     def __init__(self, chunks, length, acc, split, inward, middle, last, send, recv, freed, done):
         self.chunks, self.length = chunks, length
         self.levels = length // 2 - 1
-        self.slots = self.slots_of(length)
+        self.slots = send.shape[1]
         self.acc = acc
+        self.half, self.quarter = acc.shape[2] // 2, acc.shape[2] // 4
         self.landing = {"split": split, "inward": inward, "middle": middle, "last": last}
         self.send, self.recv, self.freed, self.done = send, recv, freed, done
         me = lax.axis_index("replica")
@@ -48,23 +48,20 @@
         self.second = (self.across_y, self.across_x)
         self.mid_bit = jnp.where(low, 0, 1)
 
-    @staticmethod
-    def slots_of(length):
-        return 4 + length // 2
-
     def neighbours(self):
         return [self.across_x, self.across_y, self.inner]
 
     def rows(self, lot, kind):
         bit = self.first_bit[lot]
-        mine = bit * HALF
+        half, quarter = self.half, self.quarter
+        mine = bit * half
         if kind == "other half":
-            return pl.ds(pl.multiple_of((1 - bit) * HALF, 16), HALF)
+            return pl.ds(pl.multiple_of((1 - bit) * half, 16), half)
         if kind == "half":
-            return pl.ds(pl.multiple_of(mine, 16), HALF)
+            return pl.ds(pl.multiple_of(mine, 16), half)
         if kind == "other quarter":
-            return pl.ds(pl.multiple_of(mine + (1 - self.mid_bit) * QUARTER, 16), QUARTER)
-        return pl.ds(pl.multiple_of(mine + self.mid_bit * QUARTER, 16), QUARTER)
+            return pl.ds(pl.multiple_of(mine + (1 - self.mid_bit) * quarter, 16), quarter)
+        return pl.ds(pl.multiple_of(mine + self.mid_bit * quarter, 16), quarter)
 
     def berth(self, stage, chunk):
         return lax.rem(chunk, self.landing[stage].shape[0])
@@ -151,6 +148,21 @@
         def pass_on(level, chunk):
             if level:
                 self.take("inward", "half", chunk)
+
+                @pl.when(chunk < self.chunks - 2)
+                def _():
+                    for lot in (0, 1):
+                        pl.semaphore_signal(
+                            self.freed.at[3, lot], inc=1, device_id={"replica": self.outer}, device_id_type=MESH
+                        )
+
+            if level < deep:
+
+                @pl.when(chunk >= 2)
+                def _():
+                    for lot in (0, 1):
+                        pl.semaphore_wait(self.freed.at[3, lot], 1)
+
             self.start("inward" if level < deep else "middle", chunk)
 
         def sent_inward(chunk):
@@ -192,19 +204,35 @@
                     self.copy("outward", chunk, lot).wait_send()
             self.done(chunk)
 
+        for level in range(deep + 1):
+            self.at(time, 6 + 2 * deep - level, level, functools.partial(joined, level))
+        for level in range(deep):
+            self.at(time, 5 + 2 * deep - level, level, functools.partial(back, level))
+        self.at(time, 5 + deep, deep, shared)
+        self.at(time, 4 + deep, deep, finish)
+        self.at(time, 3 + deep, deep, quarters)
+        for level in range(deep - 1, -1, -1):
+            self.at(time, 3 + level, level, sent_inward)
+        for level in range(deep, -1, -1):
+            if level:
+                self.at(time, 2 + level, level, functools.partial(pass_on, level))
+        self.at(time, 2, None, halves)
+        self.at(time, 2, 0, functools.partial(pass_on, 0))
         self.at(time, 1, None, split)
-        self.at(time, 2, None, halves)
-        for level in range(deep + 1):
-            self.at(time, 2 + level, level, functools.partial(pass_on, level))
-        for level in range(deep):
-            self.at(time, 3 + level, level, sent_inward)
-        self.at(time, 3 + deep, deep, quarters)
-        self.at(time, 4 + deep, deep, finish)
-        self.at(time, 5 + deep, deep, shared)
-        for level in range(deep - 1, -1, -1):
-            self.at(time, 5 + 2 * deep - level, level, functools.partial(back, level))
-        for level in range(deep, -1, -1):
-            self.at(time, 6 + 2 * deep - level, level, functools.partial(joined, level))
+
+
+def ladder_scratch(chunks, rows):
+    low = jnp.bfloat16
+    return [
+        pltpu.VMEM((chunks, 2, rows, LANES), low),
+        pltpu.VMEM((2, 2, rows // 2, LANES), low),
+        pltpu.VMEM((2, 2, rows // 2, LANES), low),
+        pltpu.VMEM((2, 2, rows // 4, LANES), low),
+        pltpu.VMEM((2, 2, rows // 4, LANES), low),
+        pltpu.SemaphoreType.DMA((7, 4, 2)),
+        pltpu.SemaphoreType.DMA((7, 4, 2)),
+        pltpu.SemaphoreType.REGULAR((4, 2)),
+    ]
 
 
 def last_offset(length):
@@ -574,6 +602,7 @@
 
 def back_kernel(
     chunks,
+    shorts,
     length,
     hidden_two,
     upstream,
@@ -601,30 +630,33 @@
     angle_hbm,
     block_out,
     input_out,
-    gate_out,
-    up_out,
-    down_out,
-    query_out,
-    key_out,
-    value_out,
-    out_out,
-    small_out,
+    summed_out,
+    short_out,
     acc,
     split,
     inward,
     mids,
     last,
+    send,
+    recv,
+    freed,
+    short_acc,
+    short_split,
+    short_inward,
+    short_mids,
+    short_last,
+    short_send,
+    short_recv,
+    short_freed,
     away,
     landed,
-    gate_buf,
-    up_buf,
+    pair_buf,
     down_buf,
     final,
     back,
     spare,
     turned,
-    gate_back,
-    up_back,
+    pair_back,
     product,
     product_turned,
     branch,
@@ -649,13 +681,15 @@
     pair_far,
     pair_low,
     gain_sum,
-    send,
-    recv,
-    freed,
+    out_rest,
     gsend,
     grecv,
+    short_gsend,
+    short_grecv,
+    gfree,
     load,
     store,
+    short_store,
     plain,
     psend,
     precv,
@@ -673,79 +707,34 @@
     tall = LANES // 2
     wide_blocks = width // LANES
 
-    def seat(number):
-        lot, place = divmod(number, 3)
-        return tiles + lot // 2, lot % 2, place * share
-
-    small_chunk, small_lot, small_row = seat(2 * wide_blocks + 2)
-
-    def tile_writes(chunk):
-        found = []
-        for lot in (0, 1):
-            at = pl.multiple_of(chunk * LANES + lot * half_hidden, LANES)
-            for number, goal in enumerate((gate_out, up_out)):
-                found.append(
-                    pltpu.make_async_copy(
-                        acc.at[chunk, lot, pl.ds(number * share, share)],
-                        goal.at[:, pl.ds(at, LANES)],
-                        store.at[chunk, lot, number],
-                    )
-                )
-            for block in range(wide_blocks):
-                found.append(
-                    pltpu.make_async_copy(
-                        acc.at[chunk, lot, pl.ds(2 * share + block * tall, tall)],
-                        down_out.at[
-                            pl.ds(pl.multiple_of(chunk * LANES + lot * tall, tall), tall),
-                            pl.ds(block * LANES, LANES),
-                        ],
-                        store.at[chunk, lot, 2 + block],
-                    )
-                )
-        return found
-
-    def rest_writes(chunk):
-        goals = [(out_out, block) for block in range(wide_blocks)]
-        goals += [(key_out, 0), (value_out, 0)]
-        goals += [(query_out, block) for block in range(wide_blocks)]
-        found = []
-        for number, (goal, block) in enumerate(goals):
-            where, lot, row = seat(number)
-            if where == chunk:
-                found.append(
-                    pltpu.make_async_copy(
-                        acc.at[where, lot, pl.ds(row, share)],
-                        goal.at[:, pl.ds(block * LANES, LANES)],
-                        store.at[where, lot, row // share],
-                    )
-                )
-        if chunk == small_chunk:
-            for block in range(wide_blocks):
-                found.append(
-                    pltpu.make_async_copy(
-                        acc.at[chunk, small_lot, pl.ds(small_row + block * 16, 16)],
-                        small_out.at[:, pl.ds(block * LANES, LANES)],
-                        store.at[chunk, small_lot, 2 + block],
-                    )
-                )
-        return found
+    def write(chunk):
+        return pltpu.make_async_copy(acc.at[chunk], summed_out.at[chunk], store.at[chunk])
+
+    def short_write(chunk):
+        return pltpu.make_async_copy(short_acc.at[chunk], short_out.at[chunk], short_store.at[chunk])
 
     def start_writes(chunk):
-        @pl.when(chunk < tiles)
-        def _():
-            for copy in tile_writes(chunk):
-                copy.start()
-
-        for rest in range(tiles, chunks):
-
-            @pl.when(chunk == rest)
-            def _():
-                for copy in rest_writes(rest):
-                    copy.start()
+        write(chunk).start()
+
+    def start_short_writes(chunk):
+        short_write(chunk).start()
 
     ladder = Ladder(chunks, length, acc, split, inward, mids, last, send, recv, freed, start_writes)
+    short_ladder = Ladder(
+        shorts,
+        length,
+        short_acc,
+        short_split,
+        short_inward,
+        short_mids,
+        short_last,
+        short_send,
+        short_recv,
+        short_freed,
+        start_short_writes,
+    )
     enter(ladder, partner)
-    tick = ladder.tick
+    tick, short_tick = ladder.tick, short_ladder.tick
 
     early = [
         pltpu.make_async_copy(source, goal, plain.at[number])
@@ -772,20 +761,15 @@
         found = []
         for lot in (0, 1):
             at = pl.ds(pl.multiple_of(tile * LANES + lot * half_hidden, LANES), LANES)
-            goal_columns = pl.ds(lot * LANES, LANES)
-            for side, gate_side, up_side in ((rank, gate_hbm, up_hbm), (partner, gate_other, up_other)):
-                number = len(found)
+            for side, both in ((rank, (gate_hbm, up_hbm)), (partner, (gate_other, up_other))):
                 goal_rows = pl.ds(pl.multiple_of(side * share, 16), share)
-                found.append(
-                    pltpu.make_async_copy(
-                        gate_side.at[:, at], gate_buf.at[slot, goal_rows, goal_columns], load.at[slot, number]
+                for which, source in enumerate(both):
+                    goal_columns = pl.ds((which * 2 + lot) * LANES, LANES)
+                    found.append(
+                        pltpu.make_async_copy(
+                            source.at[:, at], pair_buf.at[slot, goal_rows, goal_columns], load.at[slot, len(found)]
+                        )
                     )
-                )
-                found.append(
-                    pltpu.make_async_copy(
-                        up_side.at[:, at], up_buf.at[slot, goal_rows, goal_columns], load.at[slot, number + 1]
-                    )
-                )
         at = pl.ds(pl.multiple_of(tile * LANES, LANES), LANES)
         for side, source in ((rank, down_hbm), (partner, down_other)):
             found.append(
@@ -804,12 +788,49 @@
             device_id_type=MESH,
         )
 
-    def finish(chunk):
-        across(chunk).wait()
-        slot = lax.rem(chunk, 2)
+    def place_of(tile):
+        return lax.div(tile, 2), pl.multiple_of(lax.rem(tile, 2) * ROWS, 16)
+
+    def finish(tile):
+        across(tile).wait()
+        slot = lax.rem(tile, 2)
+        chunk, first = place_of(tile)
         for lot in (0, 1):
-            mine = acc[chunk, lot].astype(f32)
-            acc[chunk, lot] = (mine + landed[slot, lot].astype(f32)).astype(low)
+            mine = acc[chunk, lot, pl.ds(first, ROWS)].astype(f32)
+            acc[chunk, lot, pl.ds(first, ROWS)] = (mine + landed[slot, lot].astype(f32)).astype(low)
+
+    def short_across(chunk):
+        where = pl.ds(0, SHORT)
+        return pltpu.make_async_remote_copy(
+            src_ref=away.at[chunk % 2, :, where],
+            dst_ref=landed.at[chunk % 2, :, where],
+            send_sem=short_gsend.at[chunk],
+            recv_sem=short_grecv.at[chunk],
+            device_id={"group": partner},
+            device_id_type=MESH,
+        )
+
+    def short_finish(chunk):
+        short_across(chunk).wait()
+        where = pl.ds(0, SHORT)
+        for lot in (0, 1):
+            mine = short_acc[chunk, lot].astype(f32)
+            short_acc[chunk, lot] = (mine + landed[chunk % 2, lot, where].astype(f32)).astype(low)
+
+    def taken():
+        pl.semaphore_signal(gfree, inc=1, device_id={"group": partner}, device_id_type=MESH)
+
+    def short_seat(number):
+        if number < wide_blocks + 1:
+            return number // 4, number // 2 % 2, number % 2 * share
+        return shorts - 1, number - wide_blocks - 1, 0
+
+    def short_put(number, value, mine):
+        chunk, lot, row = short_seat(number)
+        if mine:
+            short_acc[chunk, lot, pl.ds(row, share)] = value.astype(low)
+        else:
+            away[chunk % 2, lot, pl.ds(row, share)] = value.astype(low)
 
     for copy in loads(0):
         copy.start()
@@ -823,12 +844,12 @@
 
     def put(target, where, value, first_row):
         for lot in (0, 1):
-            target[where, lot, pl.ds(first_row, share)] = value[:, lot * LANES : (lot + 1) * LANES].astype(low)
-
-    def put_down(target, where, value):
+            target[where, lot, pl.ds(pl.multiple_of(first_row, 16), share)] = value[:, lot * LANES : (lot + 1) * LANES].astype(low)
+
+    def put_down(target, where, value, first_row):
         for lot in (0, 1):
             for block in range(wide_blocks):
-                target[where, lot, pl.ds(2 * share + block * tall, tall)] = value[
+                target[where, lot, pl.ds(pl.multiple_of(first_row + block * tall, 16), tall)] = value[
                     lot * tall : (lot + 1) * tall, block * LANES : (block + 1) * LANES
                 ].astype(low)
 
@@ -838,8 +859,8 @@
         for number in range(blocks):
             at = slice(number * BLOCK, (number + 1) * BLOCK)
             hidden = hidden_two[at]
-            gate_pre = dot(hidden, gate_buf[slot])
-            up_pre = dot(hidden, up_buf[slot])
+            pre = dot(hidden, pair_buf[slot])
+            gate_pre, up_pre = pre[:, : 2 * LANES], pre[:, 2 * LANES :]
             grad = dot_nt(upstream[at], down_buf[slot])
             sigmoid = 1.0 / (1.0 + jnp.exp(-gate_pre))
             swish = gate_pre * sigmoid
@@ -847,19 +868,21 @@
             gate_grad = (grad * up_pre * sigmoid * (1.0 + gate_pre * (1.0 - sigmoid))).astype(low)
             up_grad = (grad * swish).astype(low)
             product[at] = unit
-            gate_back[at] = gate_grad
-            up_back[at] = up_grad
+            pair_back[at, : 2 * LANES] = gate_grad
+            pair_back[at, 2 * LANES :] = up_grad
             product_turned[:, at] = unit.T
             final[at] += dot(unit, down_buf[slot])
-            back[at] += dot_nt(gate_grad, gate_buf[slot]) + dot_nt(up_grad, up_buf[slot])
-        for owner, target, where in ((partner, away, slot), (rank, acc, tile)):
+            back[at] += dot_nt(pair_back[at], pair_buf[slot])
+        chunk, first = place_of(tile)
+        for owner, target, where, row in ((partner, away, slot, 0), (rank, acc, chunk, first)):
             some = turned[pl.ds(pl.multiple_of(owner * share, 16), share)]
-            put(target, where, dot(some, gate_back[...]), 0)
-            put(target, where, dot(some, up_back[...]), share)
+            both = dot(some, pair_back[...])
+            put(target, where, both[:, : 2 * LANES], row)
+            put(target, where, both[:, 2 * LANES :], row + share)
             some = product_turned[span(owner, LANES)]
-            put_down(target, where, dot(some, upstream[...]))
-
-    pace = 2
+            put_down(target, where, dot(some, upstream[...]), row + 2 * share)
+
+    beats = (2, 5, 8, 12, 15, 18)
 
     def tile_step(tile, carry):
         for copy in loads(tile):
@@ -878,18 +901,21 @@
 
         across(tile).start()
 
-        @pl.when(lax.rem(tile, pace) == pace - 1)
+        now, due = jnp.int32(1), tile < 0
+        for beat in beats:
+            now = now + (tile > beat).astype(jnp.int32)
+            due = due | (tile == beat)
+
+        @pl.when(due)
         def _():
-            tick(lax.div(tile, pace))
+            tick(now)
 
         return carry
 
     lax.fori_loop(0, tiles, tile_step, 0)
-    clock = tiles // pace
+    clock = 1 + len(beats)
 
     finish(tiles - 1)
-    tick(clock)
-    clock += 1
     for copy in early:
         copy.wait()
     gain_sum[...] = jnp.zeros_like(gain_sum)
@@ -916,18 +942,21 @@
     tick(clock)
     clock += 1
 
-    def scatter(first, values_of, target, owner_is_me):
-        for block in range(values_of.shape[1] // LANES):
-            where, lot, row = seat(first + block)
-            slot = where if owner_is_me else where % 2
-            target[slot, lot, pl.ds(row, share)] = values_of[:, block * LANES : (block + 1) * LANES].astype(low)
-
     both_sides = ((partner, away, False), (rank, acc, True))
 
     for owner, target, mine in both_sides:
         some = heads_turned[pl.ds(pl.multiple_of(owner * share, 16), share)]
-        lot_columns = (wide_blocks - 1) * LANES
-        scatter(0, dot(some, branch[:, :lot_columns]), target, mine)
+        terms = dot(some, branch[...])
+        where, row = (tiles // 2, ROWS) if mine else (tiles % 2, 0)
+        for block in range(wide_blocks - 1):
+            lot, place = divmod(block, 3)
+            target[where, lot, pl.ds(row + place * share, share)] = terms[
+                :, block * LANES : (block + 1) * LANES
+            ].astype(low)
+        if mine:
+            short_put(0, terms[:, (wide_blocks - 1) * LANES :], True)
+        else:
+            out_rest[...] = terms[:, (wide_blocks - 1) * LANES :].astype(low)
     across(tiles).start()
     finished_grad = dot_nt(square[...], branch[...]).astype(low)
     for head in range(H):
@@ -941,17 +970,15 @@
             at = slice(block * BLOCK, (block + 1) * BLOCK)
             heads_grad[group * blocks + block, :, lanes] = some[:, at]
             delta[group * blocks + block, :, lanes] = overlap[:, at]
-    last_out = LANES * (wide_blocks - 1)
     next_mat = pltpu.make_async_copy(query_hbm, square, plain.at[1])
     next_mat.start()
     next_turned = pltpu.make_async_copy(turned_hbm, hidden_turned, plain.at[2])
     next_turned.start()
-    tick(clock)
-    clock += 1
     block_write.wait()
     tokens_load = pltpu.make_async_copy(tokens_hbm, tokens, plain.at[0])
     tokens_load.start()
     finish(tiles)
+    taken()
     pair_sum[...] = jnp.zeros_like(pair_sum)
 
     key_place = lax.broadcasted_iota(jnp.int32, (BLOCK, BLOCK), 0)
@@ -979,7 +1006,7 @@
         pair_sum[0, rows_of, at] += dot_nt(queries[index], score_grad[...])
         query_sum[...] += dot(keys_turned[rows_of, at], score_grad[...])
 
-    beat = 4
+    beat = 10
 
     def attend_step(step, carry):
         group, inside = lax.div(step, per_group), lax.rem(step, per_group)
@@ -1040,11 +1067,17 @@
     tokens_load.wait()
     tick(clock)
     clock += 1
-    for owner, target, mine in both_sides:
+    short_put(0, out_rest[...], False)
+    for owner, _, mine in both_sides:
         some = hidden_turned[pl.ds(pl.multiple_of(owner * share, 16), share)]
-        scatter(wide_blocks + 2, dot_nt(some, turned[...]), target, mine)
-        some = heads_turned[pl.ds(pl.multiple_of(owner * share, 16), share)]
-        scatter(wide_blocks - 1, dot(some, branch[:, last_out:]), target, mine)
+        terms = dot_nt(some, turned[...])
+        for block in range(wide_blocks):
+            short_put(1 + block, terms[:, block * LANES : (block + 1) * LANES], mine)
+        if not mine:
+            pl.semaphore_wait(gfree, 1)
+            for chunk in range(shorts - 1):
+                short_across(chunk).start()
+    short_clock = 0
 
     @pl.when(rank == 0)
     def _():
@@ -1056,11 +1089,15 @@
         at = slice(head * HD, (head + 1) * HD)
         pair_low[0, at] = turn_back(pair_sum[0, at, own], angles[0], angles[1]).astype(low)
     pair_low[1] = pair_sum[1, :, own].astype(low)
-    for owner, target, mine in both_sides:
+    short_finish(0)
+    taken()
+    short_tick(0)
+    for owner, _, mine in both_sides:
         some = hidden_turned[pl.ds(pl.multiple_of(owner * share, 16), share)]
-        scatter(wide_blocks, dot_nt(some, pair_low[0]), target, mine)
-        scatter(wide_blocks + 1, dot_nt(some, pair_low[1]), target, mine)
-    across(tiles + 1).start()
+        short_put(wide_blocks + 1, dot_nt(some, pair_low[0]), mine)
+        short_put(wide_blocks + 2, dot_nt(some, pair_low[1]), mine)
+    short_finish(1)
+    short_tick(1)
     tick(clock)
     clock += 1
 
@@ -1095,22 +1132,24 @@
     small = jnp.where(line == 1, query_bias, small)
     small = jnp.where(line == 2, pair_bias, small)
     small = jnp.where(line == 3, gain_sum[0:1], small).astype(low)
-    finish(tiles + 1)
-    left = small_row + 16 * wide_blocks
-    for target, slot in ((away, small_chunk % 2), (acc, small_chunk)):
+    for target, where in ((short_acc, shorts - 1), (away, (shorts - 1) % 2)):
+        target[where, :, pl.ds(share, SHORT - share)] = jnp.zeros((2, SHORT - share, LANES), low)
         for block in range(wide_blocks):
-            target[slot, small_lot, pl.ds(small_row + 16 * block, 16)] = small[:, block * LANES : (block + 1) * LANES]
-        target[slot, small_lot, pl.ds(left, ROWS - left)] = jnp.zeros((ROWS - left, LANES), low)
-    across(tiles + 2).start()
+            target[where, 0, pl.ds(share + 16 * block, 16)] = small[:, block * LANES : (block + 1) * LANES]
+    pl.semaphore_wait(gfree, 1)
+    short_across(shorts - 1).start()
+    for chunk in range(2, shorts):
+        short_finish(chunk)
+        short_tick(chunk)
     tick(clock)
     clock += 1
-    finish(tiles + 2)
-
-    def remaining(time, carry):
-        tick(time)
+
+    def remaining(step, carry):
+        tick(clock + step)
+        short_tick(shorts + step)
         return carry
 
-    lax.fori_loop(clock, chunks + last_offset(length), remaining, 0)
+    lax.fori_loop(0, last_offset(length), remaining, 0)
     input_write.wait()
 
     @pl.when(rank == 1)
@@ -1118,14 +1157,12 @@
         pair_push.wait_send()
 
     def drain(chunk, carry):
-        for copy in tile_writes(chunk):
-            copy.wait()
+        write(chunk).wait()
         return carry
 
-    lax.fori_loop(0, tiles, drain, 0)
-    for chunk in range(tiles, chunks):
-        for copy in rest_writes(chunk):
-            copy.wait()
+    lax.fori_loop(0, chunks, drain, 0)
+    for chunk in range(shorts):
+        short_write(chunk).wait()
 
 
 def backward(front_parts, upstream, tokens, angles, gate_w, up_w, down_w, replicas, spread):
@@ -1152,9 +1189,9 @@
     rows, width = hidden_two.shape
     columns = gate_w.shape[1]
     tiles = columns // (2 * LANES)
-    chunks = tiles + 3
+    chunks = (tiles + 1) // 2
+    shorts = 3
     length = replicas // 4
-    slots = Ladder.slots_of(length)
     low, f32 = jnp.bfloat16, jnp.float32
     pair = 2 * LANES
     kv_width = KVH * HD
@@ -1188,38 +1225,27 @@
         angles,
     )
     return pl.pallas_call(
-        functools.partial(back_kernel, chunks, length),
+        functools.partial(back_kernel, chunks, shorts, length),
         out_shape=(
             shape((rows, width), low),
             shape((rows, width), f32),
-            shape((width // 2, columns), low),
-            shape((width // 2, columns), low),
-            shape((columns // 2, width), low),
-            shape((width // 2, H * HD), low),
-            shape((width // 2, kv_width), low),
-            shape((width // 2, kv_width), low),
-            shape((H * HD // 2, width), low),
-            shape((16, width), low),
+            shape((chunks, 2, 2 * ROWS, LANES), low),
+            shape((shorts, 2, SHORT, LANES), low),
         ),
         in_specs=[vmem] * 3 + [anywhere] * (len(inputs) - 3),
-        out_specs=(anywhere,) * 10,
+        out_specs=(anywhere,) * 4,
         scratch_shapes=[
-            pltpu.VMEM((chunks, 2, ROWS, LANES), low),
-            pltpu.VMEM((4, 2, HALF, LANES), low),
-            pltpu.VMEM((slots, 2, HALF, LANES), low),
-            pltpu.VMEM((4, 2, QUARTER, LANES), low),
-            pltpu.VMEM((4, 2, QUARTER, LANES), low),
+            *ladder_scratch(chunks, 2 * ROWS),
+            *ladder_scratch(shorts, SHORT),
             pltpu.VMEM((2, 2, ROWS, LANES), low),
             pltpu.VMEM((2, 2, ROWS, LANES), low),
-            pltpu.VMEM((2, width, pair), low),
-            pltpu.VMEM((2, width, pair), low),
+            pltpu.VMEM((2, width, 2 * pair), low),
             pltpu.VMEM((2, pair, width), low),
             pltpu.VMEM((rows, width), f32),
             pltpu.VMEM((rows, width), f32),
             pltpu.VMEM((rows, width), f32),
             pltpu.VMEM((width, rows), low),
-            pltpu.VMEM((rows, pair), low),
-            pltpu.VMEM((rows, pair), low),
+            pltpu.VMEM((rows, 2 * pair), low),
             pltpu.VMEM((rows, pair), low),
             pltpu.VMEM((pair, rows), low),
             pltpu.VMEM((rows, width), low),
@@ -1244,13 +1270,15 @@
             pltpu.VMEM((2, kv_width, rows), f32),
             pltpu.VMEM((2, kv_width, rows), low),
             pltpu.VMEM((8, width), f32),
-            pltpu.SemaphoreType.DMA((7, slots, 2)),
-            pltpu.SemaphoreType.DMA((7, slots, 2)),
-            pltpu.SemaphoreType.REGULAR((3, 2)),
+            pltpu.VMEM((width // 2, LANES), low),
             pltpu.SemaphoreType.DMA((2,)),
             pltpu.SemaphoreType.DMA((2,)),
+            pltpu.SemaphoreType.DMA((shorts,)),
+            pltpu.SemaphoreType.DMA((shorts,)),
+            pltpu.SemaphoreType.REGULAR,
             pltpu.SemaphoreType.DMA((2, 10)),
-            pltpu.SemaphoreType.DMA((chunks, 2, 2 + width // LANES)),
+            pltpu.SemaphoreType.DMA((chunks,)),
+            pltpu.SemaphoreType.DMA((shorts,)),
             pltpu.SemaphoreType.DMA((12,)),
             pltpu.SemaphoreType.DMA,
             pltpu.SemaphoreType.DMA,
@@ -1261,88 +1289,178 @@
     )(*inputs)
 
 
-SLAB = 64
-
-
-def last_kernel(count, *refs):
-    sources, small, block_low, input_low = refs[:count], refs[count], refs[count + 1], refs[count + 2]
-    outs = refs[count + 3 :]
-    goals, lines, block_out, input_out = outs[:count], outs[count : count + 5], outs[count + 5], outs[count + 6]
-    rest = outs[count + 7 :]
-    narrow, wide = rest[:count], rest[count : 2 * count]
-    load, store, plain = rest[2 * count :]
+def last_kernel(
+    summed,
+    short,
+    block_low,
+    input_low,
+    gate_out,
+    up_out,
+    down_out,
+    query_out,
+    out_out,
+    key_out,
+    value_out,
+    first_gain_out,
+    query_bias_out,
+    key_bias_out,
+    value_bias_out,
+    second_gain_out,
+    block_out,
+    input_out,
+    narrow,
+    narrow_short,
+    gate,
+    up,
+    down,
+    query,
+    out,
+    key,
+    value,
+    block_held,
+    input_held,
+    load,
+    store,
+    plain,
+):
     rank = lax.axis_index("group")
+    f32 = jnp.float32
+    chunks, shorts = summed.shape[0], short.shape[0]
+    share, columns = gate_out.shape
+    width = down_out.shape[1]
+    wide_blocks = width // LANES
+    half_hidden = columns // 2
+    tiles = half_hidden // LANES
+    tall = LANES // 2
     passed = [
-        pltpu.make_async_copy(block_low, block_out, plain.at[0]),
-        pltpu.make_async_copy(input_low, input_out, plain.at[1]),
+        (
+            pltpu.make_async_copy(source, held, plain.at[2 * number]),
+            pltpu.make_async_copy(held, goal, plain.at[2 * number + 1]),
+        )
+        for number, (source, held, goal) in enumerate(
+            ((block_low, block_held, block_out), (input_low, input_held, input_out))
+        )
     ]
-    jobs = []
-    for number, source in enumerate(sources):
-        rows, columns = source.shape
-        size = SLAB * max(1, 4864 // columns)
-        for first in range(0, rows, size):
-            at = pl.ds(first, min(size, rows - first))
-            place = len(jobs)
-            jobs.append(
-                (
-                    number,
-                    first,
-                    min(size, rows - first),
-                    pltpu.make_async_copy(source.at[at], narrow[number].at[at], load.at[place]),
-                    pltpu.make_async_copy(wide[number].at[at], goals[number].at[at], store.at[place]),
-                )
-            )
-    for job in jobs:
-        job[3].start()
-    for copy in passed:
+    rest = [
+        pltpu.make_async_copy(source, goal, plain.at[4 + number])
+        for number, (source, goal) in enumerate(((query, query_out), (out, out_out), (key, key_out), (value, value_out)))
+    ]
+    short_read = pltpu.make_async_copy(short, narrow_short, plain.at[8])
+
+    def read(chunk):
+        return pltpu.make_async_copy(summed.at[chunk], narrow.at[chunk], load.at[chunk])
+
+    def writes(tile):
+        found = []
+        for lot in (0, 1):
+            at = pl.ds(pl.multiple_of(tile * LANES + lot * half_hidden, LANES), LANES)
+            for held, goal in ((gate, gate_out), (up, up_out)):
+                found.append(pltpu.make_async_copy(held.at[:, at], goal.at[:, at], store.at[tile, len(found)]))
+        at = span(tile, LANES)
+        found.append(pltpu.make_async_copy(down.at[at], down_out.at[at], store.at[tile, 4]))
+        return found
+
+    for first, _ in passed:
+        first.start()
+    for chunk in range(chunks):
+        read(chunk).start()
+    short_read.start()
+    for first, second in passed:
+        first.wait()
+        second.start()
+
+    def place(tile, carry):
+        chunk, first = lax.div(tile, 2), lax.rem(tile, 2) * ROWS
+
+        @pl.when(lax.rem(tile, 2) == 0)
+        def _():
+            read(chunk).wait()
+
+        for lot in (0, 1):
+            at = pl.ds(pl.multiple_of(tile * LANES + lot * half_hidden, LANES), LANES)
+            for number, held in enumerate((gate, up)):
+                some = pl.ds(pl.multiple_of(first + number * share, 16), share)
+                held[:, at] = narrow[chunk, lot, some].astype(f32)
+            goal_rows = pl.ds(pl.multiple_of(tile * LANES + lot * tall, tall), tall)
+            for block in range(wide_blocks):
+                some = pl.ds(pl.multiple_of(first + 2 * share + block * tall, 16), tall)
+                down[goal_rows, block * LANES : (block + 1) * LANES] = narrow[chunk, lot, some].astype(f32)
+        for copy in writes(tile):
+            copy.start()
+        return carry
+
+    lax.fori_loop(0, tiles, place, 0)
+    for block in range(wide_blocks - 1):
+        lot, seat = divmod(block, 3)
+        out[:, block * LANES : (block + 1) * LANES] = narrow[
+            chunks - 1, lot, pl.ds(ROWS + seat * share, share)
+        ].astype(f32)
+    short_read.wait()
+    for number in range(wide_blocks + 1):
+        goal, block = (out, wide_blocks - 1) if number == 0 else (query, number - 1)
+        goal[:, block * LANES : (block + 1) * LANES] = narrow_short[
+            number // 4, number // 2 % 2, pl.ds(number % 2 * share, share)
+        ].astype(f32)
+    key[...] = narrow_short[shorts - 1, 0, pl.ds(0, share)].astype(f32)
+    value[...] = narrow_short[shorts - 1, 1, pl.ds(0, share)].astype(f32)
+    for copy in rest:
         copy.start()
-    for line, (row, first, goal) in enumerate(
-        ((0, 0, lines[0]), (1, 0, lines[1]), (2, 0, lines[2]), (2, KVH * HD, lines[3]), (3, 0, lines[4]))
+    small = jnp.concatenate(
+        [narrow_short[shorts - 1, 0, pl.ds(share + 16 * block, 16)] for block in range(wide_blocks)], axis=1
+    ).astype(f32)
+    for row, first, goal in (
+        (0, 0, first_gain_out),
+        (1, 0, query_bias_out),
+        (2, 0, key_bias_out),
+        (2, KVH * HD, value_bias_out),
+        (3, 0, second_gain_out),
     ):
         size = goal.shape[0]
-        both = small[...][row : row + 1].astype(jnp.float32)
-        mine = jnp.where(rank == 0, both[:, first : first + size], both[:, first + size : first + 2 * size])
+        line = small[row : row + 1]
+        mine = jnp.where(rank == 0, line[:, first : first + size], line[:, first + size : first + 2 * size])
         goal[...] = mine.reshape(size)
-    for number, first, size, read, write in jobs:
-        read.wait()
-
-        def cast(step, carry):
-            at = pl.ds(pl.multiple_of(first + step * 32, 32), 32)
-            wide[number][at] = narrow[number][at].astype(jnp.float32)
-            return carry
-
-        lax.fori_loop(0, size // 32, cast, 0)
-        write.start()
-    for job in jobs:
-        job[4].wait()
-    for copy in passed:
+
+    def drain(tile, carry):
+        for copy in writes(tile):
+            copy.wait()
+        return carry
+
+    lax.fori_loop(0, tiles, drain, 0)
+    for copy in rest:
         copy.wait()
-
-
-def finish_outputs(sums, small, block_low, input_low, sizes):
+    for _, second in passed:
+        second.wait()
+
+
+def finish_outputs(summed, short, block_low, input_low, columns, sizes):
     low, f32 = jnp.bfloat16, jnp.float32
+    width = block_low.shape[1]
+    share, heads, kv_width = width // 2, H * HD, KVH * HD
+    tiles = columns // (2 * LANES)
     anywhere = pl.BlockSpec(memory_space=pl.ANY)
     vmem = pl.BlockSpec(memory_space=pltpu.VMEM)
     shape = jax.ShapeDtypeStruct
-    count = len(sums)
-    jobs = 0
-    for item in sums:
-        rows, columns = item.shape
-        jobs += -(-rows // (SLAB * max(1, 4864 // columns)))
+    mats = ((share, columns), (share, columns), (columns // 2, width), (share, heads), (heads // 2, width))
+    mats += ((share, kv_width), (share, kv_width))
     return pl.pallas_call(
-        functools.partial(last_kernel, count),
+        last_kernel,
         out_shape=tuple(
-            [shape(item.shape, f32) for item in sums]
+            [shape(item, f32) for item in mats]
             + [shape((size,), f32) for size in sizes]
             + [shape(block_low.shape, block_low.dtype), shape(input_low.shape, input_low.dtype)]
         ),
-        in_specs=[anywhere] * count + [vmem] + [anywhere] * 2,
-        out_specs=tuple([anywhere] * count + [vmem] * 5 + [anywhere] * 2),
-        scratch_shapes=[pltpu.VMEM(item.shape, low) for item in sums]
-        + [pltpu.VMEM(item.shape, f32) for item in sums]
-        + [pltpu.SemaphoreType.DMA((jobs,)), pltpu.SemaphoreType.DMA((jobs,)), pltpu.SemaphoreType.DMA((2,))],
-        compiler_params=pltpu.CompilerParams(vmem_limit_bytes=56 * 1024 * 1024),
-    )(*sums, small, block_low, input_low)
+        in_specs=[anywhere] * 4,
+        out_specs=tuple([anywhere] * 7 + [vmem] * 5 + [anywhere] * 2),
+        scratch_shapes=[pltpu.VMEM(summed.shape, low), pltpu.VMEM(short.shape, low)]
+        + [pltpu.VMEM(item, f32) for item in mats]
+        + [pltpu.VMEM(item.shape, item.dtype) for item in (block_low, input_low)]
+        + [
+            pltpu.SemaphoreType.DMA((summed.shape[0],)),
+            pltpu.SemaphoreType.DMA((tiles, 5)),
+            pltpu.SemaphoreType.DMA((9,)),
+        ],
+        compiler_params=pltpu.CompilerParams(vmem_limit_bytes=60 * 1024 * 1024),
+    )(summed, short, block_low, input_low)
 
 
 def local(
@@ -1381,14 +1499,8 @@
     (
         block_output,
         input_grad,
-        gate_sum,
-        up_sum,
-        down_sum,
-        query_sum,
-        key_sum,
-        value_sum,
-        out_sum,
-        small,
+        summed,
+        short,
     ) = backward(
         parts, cotangent, tokens, angles, gate_weight, up_weight, down_weight, lax.axis_size("replica"), spread
     )
@@ -1409,9 +1521,7 @@
         second_gain_grad,
         block_output,
         input_grad,
-    ) = finish_outputs(
-        (gate_sum, up_sum, down_sum, query_sum, out_sum, key_sum, value_sum), small, block_output, input_grad, sizes
-    )
+    ) = finish_outputs(summed, short, block_output, input_grad, gate_weight.shape[1], sizes)
     return (
         block_output,
         input_grad,

time: 448 us -> 349 us (0.78)
  Pallas kernels: 447 us -> 348 us
    pallas_call x2, Pallas kernels: 417 us -> 318 us  [the longest x1 300 us: backward(): pl.pallas_call(functools.partial(back_kernel, chunks, shorts, length), ou...]
where the time goes in v2:
time: 349 us
  Pallas kernels  348 us (100%)
    pallas_call x1, Pallas kernels, backward(): pl.pallas_call(functools.partial(back_kernel, chunks, shorts, length), ou...  300 us
    pallas_call x1, Pallas kernels, front(): pl.pallas_call(front_kernel, out_shape=tuple((item for item, _ in outs)),...  29.5 us
    pallas_call x1, Pallas kernels, finish_outputs(): pl.pallas_call(last_kernel, out_shape=tuple([shape(item, f32) for item in...  18.1 us

profile of v2, /device:TPU:0, one launch (start us, length us, event | category | flops | bytes accessed | tf_op | source)
XLA Modules:
  0.0 348.7 jit_solution(16988067475113460618)
XLA Ops:
  0.6 29.5 %shard_map.254 = (bf16[768,896]{1,0:T(8,128)(2,1)}, f32[768,896]{1,0:T(8,128)}, bf16[896,768]{1,0:T(8,128)(2,1)}, bf16[6,64,1792]{2,1,0:T(8,128)(2,1)}, bf16[2,1...) custom-call(bf16[768,896]{1,0:T(8,128)(2,1)} %tokens_hbm.1, ...), custom_call_target="tpu_custom_call" | custom-call | tf_op jit(solution)/shard_map/pallas_call | solution.py:570
  30.1 300.4 %shard_map.255 = (bf16[768,896]{1,0:T(8,128)(2,1)}, f32[768,896]{1,0:T(8,128)}, bf16[10,2,2688,128]{3,2,1,0:T(8,128)(2,1)}, bf16[3,2,896,128]{3,2,1,0:T(8,128)(2,1)}) custom-call(bf16[768,896]{1,0:T(8,128)(2,1)} %get-tuple-element.50.hidden_two, bf16[768,896]{1,0:T(8,128)(2,1)} %upstream.1, f32[8,896]{1,0:T(8,128)} %get-tuple-element.51.vectors, ...), custom_call_target="tpu_custom_call" | custom-call | tf_op jit(solution)/shard_map/pallas_call | solution.py:1227
  330.5 18.1 %shard_map.256 = (f32[448,4864]{1,0:T(8,128)}, f32[448,4864]{1,0:T(8,128)}, f32[2432,896]{1,0:T(8,128)}, f32[448,896]{1,0:T(8,128)}, f32[448,896]{1,0:T(8,128)},...) custom-call(bf16[10,2,2688,128]{3,2,1,0:T(8,128)(2,1)} %get-tuple-el, ...), custom_call_target="tpu_custom_call" | custom-call | tf_op jit(solution)/shard_map/pallas_call | solution.py:1445

commit v3 on v2

--- a/solution.py
+++ b/solution.py
@@ -279,6 +279,10 @@
 def turn_back(head, cosine, sine):
     top, low = head[: HD // 2], head[HD // 2 :]
     return jnp.concatenate([top * cosine + low * sine, low * cosine - top * sine], axis=0)
+
+
+def strips(total):
+    return [slice(first, min(first + 2 * LANES, total)) for first in range(0, total, 2 * LANES)]
 
 
 def span(number, size):
@@ -506,10 +510,15 @@
     pushes[4].wait_recv()
     local[3].wait()
 
+    for block in range(blocks):
+        at = slice(block * BLOCK, (block + 1) * BLOCK)
+        hidden[at] = attended_turned[:, at].T
+    for strip in strips(width):
+        wide[:, strip] = dot(hidden[...], out_mat[:, strip])
+
     def close(number, carry):
         at = span(number, BLOCK)
-        branch = dot(attended_turned[:, at].T, out_mat[...])
-        total = tokens[at].astype(f32) + branch
+        total = tokens[at].astype(f32) + wide[at]
         middle[at] = total
         inverse = lax.rsqrt(jnp.mean(total * total, axis=-1, keepdims=True) + norm_eps)
         hidden_two[at] = (total * inverse * vectors_full[4:5]).astype(low)
@@ -658,7 +667,7 @@
     turned,
     pair_back,
     product,
-    product_turned,
+    upstream_turned,
     branch,
     heads_turned,
     queries,
@@ -704,7 +713,6 @@
     blocks = rows // BLOCK
     ratio = H // KVH
     low, f32 = jnp.bfloat16, jnp.float32
-    tall = LANES // 2
     wide_blocks = width // LANES
 
     def write(chunk):
@@ -740,7 +748,6 @@
         pltpu.make_async_copy(source, goal, plain.at[number])
         for number, (source, goal) in enumerate(
             (
-                (middle_hbm, spare),
                 (queries_hbm, queries),
                 (keys_hbm, keys),
                 (values_hbm, values),
@@ -791,6 +798,9 @@
     def place_of(tile):
         return lax.div(tile, 2), pl.multiple_of(lax.rem(tile, 2) * ROWS, 16)
 
+    def partner_first(half):
+        return pl.ds(pl.multiple_of(jnp.where(rank == half, share, 0), 16), share)
+
     def finish(tile):
         across(tile).wait()
         slot = lax.rem(tile, 2)
@@ -840,47 +850,51 @@
     back[...] = jnp.zeros_like(back)
     for block in range(blocks):
         at = slice(block * BLOCK, (block + 1) * BLOCK)
-        turned[:, at] = hidden_two[at].T
-
-    def put(target, where, value, first_row):
-        for lot in (0, 1):
-            target[where, lot, pl.ds(pl.multiple_of(first_row, 16), share)] = value[:, lot * LANES : (lot + 1) * LANES].astype(low)
-
-    def put_down(target, where, value, first_row):
-        for lot in (0, 1):
-            for block in range(wide_blocks):
-                target[where, lot, pl.ds(pl.multiple_of(first_row + block * tall, 16), tall)] = value[
-                    lot * tall : (lot + 1) * tall, block * LANES : (block + 1) * LANES
-                ].astype(low)
+        block_turned = hidden_two[at].T
+        for half in (0, 1):
+            turned[partner_first(half), at] = block_turned[half * share : (half + 1) * share]
+        upstream_turned[:, at] = upstream[at].T
+
+    def halves_of(value, axis):
+        cut = value.shape[axis] // 2
+        first, second = (value[:cut], value[cut:]) if axis == 0 else (value[:, :cut], value[:, cut:])
+        return jnp.where(rank == 0, second, first), jnp.where(rank == 0, first, second)
+
+    def put(target, where, lot, first_row, value):
+        target[where, lot, pl.ds(pl.multiple_of(first_row, 16), share)] = value.astype(low)
 
     def compute(tile):
         slot = lax.rem(tile, 2)
-
-        for number in range(blocks):
-            at = slice(number * BLOCK, (number + 1) * BLOCK)
-            hidden = hidden_two[at]
-            pre = dot(hidden, pair_buf[slot])
-            gate_pre, up_pre = pre[:, : 2 * LANES], pre[:, 2 * LANES :]
-            grad = dot_nt(upstream[at], down_buf[slot])
+        chunk, first = place_of(tile)
+        for strip in strips(4 * LANES):
+            spare[:, strip] = dot(hidden_two[...], pair_buf[slot, :, strip])
+        spare[:, 4 * LANES : 6 * LANES] = dot_nt(upstream[...], down_buf[slot])
+
+        def middle_part(number, carry):
+            at = span(number, BLOCK)
+            gate_pre, up_pre = spare[at, : 2 * LANES], spare[at, 2 * LANES : 4 * LANES]
+            grad = spare[at, 4 * LANES : 6 * LANES]
             sigmoid = 1.0 / (1.0 + jnp.exp(-gate_pre))
             swish = gate_pre * sigmoid
-            unit = (swish * up_pre).astype(low)
-            gate_grad = (grad * up_pre * sigmoid * (1.0 + gate_pre * (1.0 - sigmoid))).astype(low)
-            up_grad = (grad * swish).astype(low)
-            product[at] = unit
-            pair_back[at, : 2 * LANES] = gate_grad
-            pair_back[at, 2 * LANES :] = up_grad
-            product_turned[:, at] = unit.T
-            final[at] += dot(unit, down_buf[slot])
-            back[at] += dot_nt(pair_back[at], pair_buf[slot])
-        chunk, first = place_of(tile)
-        for owner, target, where, row in ((partner, away, slot, 0), (rank, acc, chunk, first)):
-            some = turned[pl.ds(pl.multiple_of(owner * share, 16), share)]
-            both = dot(some, pair_back[...])
-            put(target, where, both[:, : 2 * LANES], row)
-            put(target, where, both[:, 2 * LANES :], row + share)
-            some = product_turned[span(owner, LANES)]
-            put_down(target, where, dot(some, upstream[...]), row + 2 * share)
+            product[at] = (swish * up_pre).astype(low)
+            pair_back[at, : 2 * LANES] = (grad * up_pre * sigmoid * (1.0 + gate_pre * (1.0 - sigmoid))).astype(low)
+            pair_back[at, 2 * LANES :] = (grad * swish).astype(low)
+            return carry
+
+        lax.fori_loop(0, blocks, middle_part, 0)
+        for strip in strips(width):
+            final[:, strip] += dot(product[...], down_buf[slot, :, strip])
+        for strip in strips(width):
+            back[:, strip] += dot_nt(pair_back[...], pair_buf[slot, strip])
+        sides = ((away, slot, 0), (acc, chunk, first))
+        for which, strip in enumerate(strips(4 * LANES)):
+            both = dot(turned[...], pair_back[:, strip])
+            for (target, where, row), term in zip(sides, (both[:share], both[share:])):
+                for lot in (0, 1):
+                    put(target, where, lot, row + which * share, term[:, lot * LANES : (lot + 1) * LANES])
+        for (target, where, row), term in zip(sides, halves_of(dot(upstream_turned[...], product[...]), 1)):
+            for lot in (0, 1):
+                put(target, where, lot, row + 2 * share, term[lot * share : (lot + 1) * share])
 
     beats = (2, 5, 8, 12, 15, 18)
 
@@ -915,9 +929,12 @@
     lax.fori_loop(0, tiles, tile_step, 0)
     clock = 1 + len(beats)
 
+    middle_load = pltpu.make_async_copy(middle_hbm, spare, plain.at[11])
+    middle_load.start()
     finish(tiles - 1)
     for copy in early:
         copy.wait()
+    middle_load.wait()
     gain_sum[...] = jnp.zeros_like(gain_sum)
 
     def norm_two(number, carry):
@@ -942,38 +959,43 @@
     tick(clock)
     clock += 1
 
-    both_sides = ((partner, away, False), (rank, acc, True))
-
-    for owner, target, mine in both_sides:
+    sides = ((away, tiles % 2, 0), (acc, tiles // 2, ROWS))
+    for (target, where, row), owner in zip(sides, (partner, rank)):
         some = heads_turned[pl.ds(pl.multiple_of(owner * share, 16), share)]
-        terms = dot(some, branch[...])
-        where, row = (tiles // 2, ROWS) if mine else (tiles % 2, 0)
-        for block in range(wide_blocks - 1):
-            lot, place = divmod(block, 3)
-            target[where, lot, pl.ds(row + place * share, share)] = terms[
-                :, block * LANES : (block + 1) * LANES
-            ].astype(low)
-        if mine:
-            short_put(0, terms[:, (wide_blocks - 1) * LANES :], True)
-        else:
-            out_rest[...] = terms[:, (wide_blocks - 1) * LANES :].astype(low)
+        for strip in strips(width):
+            term = dot(some, branch[:, strip])
+            for inside in range(term.shape[1] // LANES):
+                block = strip.start // LANES + inside
+                lot, seat = divmod(block, 3)
+                piece = term[:, inside * LANES : (inside + 1) * LANES]
+                if block < wide_blocks - 1:
+                    put(target, where, lot, row + seat * share, piece)
+                elif target is acc:
+                    short_put(0, piece, True)
+                else:
+                    out_rest[...] = piece.astype(low)
     across(tiles).start()
-    finished_grad = dot_nt(square[...], branch[...]).astype(low)
-    for head in range(H):
-        group, place = divmod(head, ratio)
-        lanes = slice(place * BLOCK, (place + 1) * BLOCK)
-        some = finished_grad[head * HD : (head + 1) * HD]
-        features = slice(head * HD, (head + 1) * HD)
-        result = heads_turned[features].astype(f32) + hidden_turned[features].astype(f32)
-        overlap = jnp.sum(some.astype(f32) * result, axis=0, keepdims=True)
-        for block in range(blocks):
-            at = slice(block * BLOCK, (block + 1) * BLOCK)
-            heads_grad[group * blocks + block, :, lanes] = some[:, at]
-            delta[group * blocks + block, :, lanes] = overlap[:, at]
+    for block in range(blocks):
+        at = slice(block * BLOCK, (block + 1) * BLOCK)
+        finished_grad = dot_nt(square[...], branch[at]).astype(low)
+        for head in range(H):
+            group, place = divmod(head, ratio)
+            lanes = slice(place * BLOCK, (place + 1) * BLOCK)
+            features = slice(head * HD, (head + 1) * HD)
+            some = finished_grad[features]
+            result = heads_turned[features, at].astype(f32) + hidden_turned[features, at].astype(f32)
+            heads_grad[group * blocks + block, :, lanes] = some
+            delta[group * blocks + block, :, lanes] = jnp.sum(some.astype(f32) * result, axis=0, keepdims=True)
     next_mat = pltpu.make_async_copy(query_hbm, square, plain.at[1])
     next_mat.start()
-    next_turned = pltpu.make_async_copy(turned_hbm, hidden_turned, plain.at[2])
-    next_turned.start()
+    next_turned = [
+        pltpu.make_async_copy(
+            turned_hbm.at[pl.ds(half * share, share)], hidden_turned.at[partner_first(half)], plain.at[2 + half]
+        )
+        for half in (0, 1)
+    ]
+    for copy in next_turned:
+        copy.start()
     block_write.wait()
     tokens_load = pltpu.make_async_copy(tokens_hbm, tokens, plain.at[0])
     tokens_load.start()
@@ -1001,10 +1023,10 @@
         weights_grad = dot(values[group, at], heads_grad[index])
         probs[...] = weights.astype(low)
         score_grad[...] = (weights * (weights_grad - delta[index])).astype(low)
-        rows_of = span(group, HD)
-        pair_sum[1, rows_of, at] += dot_nt(heads_grad[index], probs[...])
-        pair_sum[0, rows_of, at] += dot_nt(queries[index], score_grad[...])
-        query_sum[...] += dot(keys_turned[rows_of, at], score_grad[...])
+        pair_sum[group, at] += jnp.concatenate(
+            [dot_nt(score_grad[...], queries[index]), dot_nt(probs[...], heads_grad[index])], axis=1
+        )
+        query_sum[...] += dot(keys_turned[span(group, HD), at], score_grad[...])
 
     beat = 10
 
@@ -1050,7 +1072,7 @@
     clock += steps // beat
 
     pair_push = pltpu.make_async_remote_copy(
-        src_ref=pair_sum.at[:, :, pl.ds(0, rows)],
+        src_ref=pair_sum.at[:, pl.ds(0, rows)],
         dst_ref=pair_far,
         send_sem=psend,
         recv_sem=precv,
@@ -1063,48 +1085,59 @@
         pair_push.start()
 
     next_mat.wait()
-    next_turned.wait()
+    for copy in next_turned:
+        copy.wait()
     tokens_load.wait()
     tick(clock)
     clock += 1
     short_put(0, out_rest[...], False)
-    for owner, _, mine in both_sides:
-        some = hidden_turned[pl.ds(pl.multiple_of(owner * share, 16), share)]
-        terms = dot_nt(some, turned[...])
-        for block in range(wide_blocks):
-            short_put(1 + block, terms[:, block * LANES : (block + 1) * LANES], mine)
-        if not mine:
-            pl.semaphore_wait(gfree, 1)
-            for chunk in range(shorts - 1):
-                short_across(chunk).start()
-    short_clock = 0
+    for strip in strips(width):
+        terms = dot_nt(hidden_turned[...], turned[strip])
+        for inside in range(terms.shape[1] // LANES):
+            piece = terms[:, inside * LANES : (inside + 1) * LANES]
+            block = strip.start // LANES + inside
+            short_put(1 + block, piece[:share], False)
+            short_put(1 + block, piece[share:], True)
+    pl.semaphore_wait(gfree, 1)
+    for chunk in range(shorts - 1):
+        short_across(chunk).start()
 
     @pl.when(rank == 0)
     def _():
         pair_push.wait_recv()
-        pair_sum[:, :, :rows] += pair_far[...]
+        pair_sum[:, :rows] += pair_far[...]
 
     own = span(rank, rows)
     for head in range(KVH):
         at = slice(head * HD, (head + 1) * HD)
-        pair_low[0, at] = turn_back(pair_sum[0, at, own], angles[0], angles[1]).astype(low)
-    pair_low[1] = pair_sum[1, :, own].astype(low)
+        both = pair_sum[head, own].T
+        pair_low[0, at] = turn_back(both[:HD], angles[0], angles[1]).astype(low)
+        pair_low[1, at] = both[HD:].astype(low)
     short_finish(0)
     taken()
     short_tick(0)
-    for owner, _, mine in both_sides:
-        some = hidden_turned[pl.ds(pl.multiple_of(owner * share, 16), share)]
-        short_put(wide_blocks + 1, dot_nt(some, pair_low[0]), mine)
-        short_put(wide_blocks + 2, dot_nt(some, pair_low[1]), mine)
+    for number in (0, 1):
+        terms = dot_nt(hidden_turned[...], pair_low[number])
+        for term, mine in ((terms[:share], False), (terms[share:], True)):
+            short_put(wide_blocks + 1 + number, term, mine)
     short_finish(1)
     short_tick(1)
     tick(clock)
     clock += 1
 
+    for block in range(blocks):
+        at = slice(block * BLOCK, (block + 1) * BLOCK)
+        branch[at] = turned[:, at].T
+    for strip in strips(width):
+        final[:, strip] = (
+            dot_nt(branch[...], square[strip])
+            + dot_nt(pair_low[0].T, key_mat[strip])
+            + dot_nt(pair_low[1].T, value_mat[strip])
+        )
+
     def norm_one(number, carry):
         at = span(number, BLOCK)
-        grad = dot_nt(turned[:, at].T, square[...])
-        grad += dot_nt(pair_low[0, :, at].T, key_mat[...]) + dot_nt(pair_low[1, :, at].T, value_mat[...])
+        grad = final[at]
         residual = tokens[at].astype(f32)
         inverse = lax.rsqrt(jnp.mean(residual * residual, axis=-1, keepdims=True) + norm_eps)
         normed = residual * inverse
@@ -1247,7 +1280,7 @@
             pltpu.VMEM((width, rows), low),
             pltpu.VMEM((rows, 2 * pair), low),
             pltpu.VMEM((rows, pair), low),
-            pltpu.VMEM((pair, rows), low),
+            pltpu.VMEM((width, rows), low),
             pltpu.VMEM((rows, width), low),
             pltpu.VMEM((H * HD, rows), low),
             pltpu.VMEM(queries.shape, low),
@@ -1266,8 +1299,8 @@
             pltpu.VMEM((BLOCK, queries.shape[2]), low),
             pltpu.VMEM((BLOCK, queries.shape[2]), low),
             pltpu.VMEM(queries.shape[1:], f32),
-            pltpu.VMEM((2, kv_width, rows * spread), f32),
-            pltpu.VMEM((2, kv_width, rows), f32),
+            pltpu.VMEM((KVH, rows * spread, 2 * HD), f32),
+            pltpu.VMEM((KVH, rows, 2 * HD), f32),
             pltpu.VMEM((2, kv_width, rows), low),
             pltpu.VMEM((8, width), f32),
             pltpu.VMEM((width // 2, LANES), low),
@@ -1331,7 +1364,6 @@
     wide_blocks = width // LANES
     half_hidden = columns // 2
     tiles = half_hidden // LANES
-    tall = LANES // 2
     passed = [
         (
             pltpu.make_async_copy(source, held, plain.at[2 * number]),
@@ -1381,10 +1413,9 @@
             for number, held in enumerate((gate, up)):
                 some = pl.ds(pl.multiple_of(first + number * share, 16), share)
                 held[:, at] = narrow[chunk, lot, some].astype(f32)
-            goal_rows = pl.ds(pl.multiple_of(tile * LANES + lot * tall, tall), tall)
-            for block in range(wide_blocks):
-                some = pl.ds(pl.multiple_of(first + 2 * share + block * tall, 16), tall)
-                down[goal_rows, block * LANES : (block + 1) * LANES] = narrow[chunk, lot, some].astype(f32)
+        some = pl.ds(pl.multiple_of(first + 2 * share, 16), share)
+        both = jnp.concatenate([narrow[chunk, lot, some] for lot in (0, 1)], axis=0)
+        down[span(tile, LANES)] = both.T.astype(f32)
         for copy in writes(tile):
             copy.start()
         return carry

time: 349 us -> 361 us (1.034)
  Pallas kernels: 348 us -> 360 us
    pallas_call x1, Pallas kernels: 300 us -> 312 us  [backward(): pl.pallas_call(functools.partial(back_kernel, chunks, shorts, length), ou...]
where the time goes in v3:
time: 361 us
  Pallas kernels  360 us (100%)
    pallas_call x1, Pallas kernels, backward(): pl.pallas_call(functools.partial(back_kernel, chunks, shorts, length), ou...  312 us
    pallas_call x1, Pallas kernels, front(): pl.pallas_call(front_kernel, out_shape=tuple((item for item, _ in outs)),...  29.5 us
    pallas_call x1, Pallas kernels, finish_outputs(): pl.pallas_call(last_kernel, out_shape=tuple([shape(item, f32) for item in...  18.1 us

profile of v3, /device:TPU:0, one launch (start us, length us, event | category | flops | bytes accessed | tf_op | source)
XLA Modules:
  0.0 360.6 jit_solution(15476714812022238044)
XLA Ops:
  0.6 29.5 %shard_map.254 = (bf16[768,896]{1,0:T(8,128)(2,1)}, f32[768,896]{1,0:T(8,128)}, bf16[896,768]{1,0:T(8,128)(2,1)}, bf16[6,64,1792]{2,1,0:T(8,128)(2,1)}, bf16[2,1...) custom-call(bf16[768,896]{1,0:T(8,128)(2,1)} %tokens_hbm.1, ...), custom_call_target="tpu_custom_call" | custom-call | tf_op jit(solution)/shard_map/pallas_call | solution.py:579
  30.1 312.2 %shard_map.255 = (bf16[768,896]{1,0:T(8,128)(2,1)}, f32[768,896]{1,0:T(8,128)}, bf16[10,2,2688,128]{3,2,1,0:T(8,128)(2,1)}, bf16[3,2,896,128]{3,2,1,0:T(8,128)(2,1)}) custom-call(bf16[768,896]{1,0:T(8,128)(2,1)} %get-tuple-element.50.hidden_two, bf16[768,896]{1,0:T(8,128)(2,1)} %upstream.1, f32[8,896]{1,0:T(8,128)} %get-tuple-element.51.vectors, ...), custom_call_target="tpu_custom_call" | custom-call | tf_op jit(solution)/shard_map/pallas_call | solution.py:1260
  342.3 18.1 %shard_map.256 = (f32[448,4864]{1,0:T(8,128)}, f32[448,4864]{1,0:T(8,128)}, f32[2432,896]{1,0:T(8,128)}, f32[448,896]{1,0:T(8,128)}, f32[448,896]{1,0:T(8,128)},...) custom-call(bf16[10,2,2688,128]{3,2,1,0:T(8,128)(2,1)} %get-tuple-el, ...), custom_call_target="tpu_custom_call" | custom-call | tf_op jit(solution)/shard_map/pallas_call | solution.py:1476

commit v4 on v1

--- a/solution.py
+++ b/solution.py
@@ -226,6 +226,7 @@
 
 
 BLOCK = 256
+AHEAD = 2
 
 
 def dot(left, right):
@@ -768,7 +769,7 @@
     ]
 
     def loads(tile):
-        slot = lax.rem(tile, 2)
+        slot = lax.rem(tile, AHEAD + 1)
         found = []
         for lot in (0, 1):
             at = pl.ds(pl.multiple_of(tile * LANES + lot * half_hidden, LANES), LANES)
@@ -811,8 +812,9 @@
             mine = acc[chunk, lot].astype(f32)
             acc[chunk, lot] = (mine + landed[slot, lot].astype(f32)).astype(low)
 
-    for copy in loads(0):
-        copy.start()
+    for tile in range(AHEAD):
+        for copy in loads(tile):
+            copy.start()
     for copy in early:
         copy.start()
     final[...] = jnp.zeros_like(final)
@@ -833,14 +835,14 @@
                 ].astype(low)
 
     def compute(tile):
-        slot = lax.rem(tile, 2)
+        slot, seat_of = lax.rem(tile, 2), lax.rem(tile, AHEAD + 1)
 
         for number in range(blocks):
             at = slice(number * BLOCK, (number + 1) * BLOCK)
             hidden = hidden_two[at]
-            gate_pre = dot(hidden, gate_buf[slot])
-            up_pre = dot(hidden, up_buf[slot])
-            grad = dot_nt(upstream[at], down_buf[slot])
+            gate_pre = dot(hidden, gate_buf[seat_of])
+            up_pre = dot(hidden, up_buf[seat_of])
+            grad = dot_nt(upstream[at], down_buf[seat_of])
             sigmoid = 1.0 / (1.0 + jnp.exp(-gate_pre))
             swish = gate_pre * sigmoid
             unit = (swish * up_pre).astype(low)
@@ -850,8 +852,8 @@
             gate_back[at] = gate_grad
             up_back[at] = up_grad
             product_turned[:, at] = unit.T
-            final[at] += dot(unit, down_buf[slot])
-            back[at] += dot_nt(gate_grad, gate_buf[slot]) + dot_nt(up_grad, up_buf[slot])
+            final[at] += dot(unit, down_buf[seat_of])
+            back[at] += dot_nt(gate_grad, gate_buf[seat_of]) + dot_nt(up_grad, up_buf[seat_of])
         for owner, target, where in ((partner, away, slot), (rank, acc, tile)):
             some = turned[pl.ds(pl.multiple_of(owner * share, 16), share)]
             put(target, where, dot(some, gate_back[...]), 0)
@@ -859,15 +861,15 @@
             some = product_turned[span(owner, LANES)]
             put_down(target, where, dot(some, upstream[...]))
 
-    pace = 2
+    paced = 12
 
     def tile_step(tile, carry):
         for copy in loads(tile):
             copy.wait()
 
-        @pl.when(tile + 1 < tiles)
+        @pl.when(tile + AHEAD < tiles)
         def _():
-            for copy in loads(tile + 1):
+            for copy in loads(tile + AHEAD):
                 copy.start()
 
         compute(tile)
@@ -878,18 +880,18 @@
 
         across(tile).start()
 
-        @pl.when(lax.rem(tile, pace) == pace - 1)
+        before, after = lax.div(tile * paced, tiles), lax.div((tile + 1) * paced, tiles)
+
+        @pl.when(after > before)
         def _():
-            tick(lax.div(tile, pace))
+            tick(before)
 
         return carry
 
     lax.fori_loop(0, tiles, tile_step, 0)
-    clock = tiles // pace
+    clock = paced
 
     finish(tiles - 1)
-    tick(clock)
-    clock += 1
     for copy in early:
         copy.wait()
     gain_sum[...] = jnp.zeros_like(gain_sum)
@@ -946,8 +948,6 @@
     next_mat.start()
     next_turned = pltpu.make_async_copy(turned_hbm, hidden_turned, plain.at[2])
     next_turned.start()
-    tick(clock)
-    clock += 1
     block_write.wait()
     tokens_load = pltpu.make_async_copy(tokens_hbm, tokens, plain.at[0])
     tokens_load.start()
@@ -979,7 +979,7 @@
         pair_sum[0, rows_of, at] += dot_nt(queries[index], score_grad[...])
         query_sum[...] += dot(keys_turned[rows_of, at], score_grad[...])
 
-    beat = 4
+    beat = 5
 
     def attend_step(step, carry):
         group, inside = lax.div(step, per_group), lax.rem(step, per_group)
@@ -1211,9 +1211,9 @@
             pltpu.VMEM((4, 2, QUARTER, LANES), low),
             pltpu.VMEM((2, 2, ROWS, LANES), low),
             pltpu.VMEM((2, 2, ROWS, LANES), low),
-            pltpu.VMEM((2, width, pair), low),
-            pltpu.VMEM((2, width, pair), low),
-            pltpu.VMEM((2, pair, width), low),
+            pltpu.VMEM((AHEAD + 1, width, pair), low),
+            pltpu.VMEM((AHEAD + 1, width, pair), low),
+            pltpu.VMEM((AHEAD + 1, pair, width), low),
             pltpu.VMEM((rows, width), f32),
             pltpu.VMEM((rows, width), f32),
             pltpu.VMEM((rows, width), f32),
@@ -1249,7 +1249,7 @@
             pltpu.SemaphoreType.REGULAR((3, 2)),
             pltpu.SemaphoreType.DMA((2,)),
             pltpu.SemaphoreType.DMA((2,)),
-            pltpu.SemaphoreType.DMA((2, 10)),
+            pltpu.SemaphoreType.DMA((AHEAD + 1, 10)),
             pltpu.SemaphoreType.DMA((chunks, 2, 2 + width // LANES)),
             pltpu.SemaphoreType.DMA((12,)),
             pltpu.SemaphoreType.DMA,
@@ -1270,11 +1270,13 @@
     goals, lines, block_out, input_out = outs[:count], outs[count : count + 5], outs[count + 5], outs[count + 6]
     rest = outs[count + 7 :]
     narrow, wide = rest[:count], rest[count : 2 * count]
-    load, store, plain = rest[2 * count :]
+    block_held, input_held, load, store, plain = rest[2 * count :]
     rank = lax.axis_index("group")
     passed = [
-        pltpu.make_async_copy(block_low, block_out, plain.at[0]),
-        pltpu.make_async_copy(input_low, input_out, plain.at[1]),
+        (pltpu.make_async_copy(source, held, plain.at[2 * number]), pltpu.make_async_copy(held, goal, plain.at[2 * number + 1]))
+        for number, (source, held, goal) in enumerate(
+            ((block_low, block_held, block_out), (input_low, input_held, input_out))
+        )
     ]
     jobs = []
     for number, source in enumerate(sources):
@@ -1292,10 +1294,10 @@
                     pltpu.make_async_copy(wide[number].at[at], goals[number].at[at], store.at[place]),
                 )
             )
+    for read, _ in passed:
+        read.start()
     for job in jobs:
         job[3].start()
-    for copy in passed:
-        copy.start()
     for line, (row, first, goal) in enumerate(
         ((0, 0, lines[0]), (1, 0, lines[1]), (2, 0, lines[2]), (2, KVH * HD, lines[3]), (3, 0, lines[4]))
     ):
@@ -1303,6 +1305,9 @@
         both = small[...][row : row + 1].astype(jnp.float32)
         mine = jnp.where(rank == 0, both[:, first : first + size], both[:, first + size : first + 2 * size])
         goal[...] = mine.reshape(size)
+    for read, write in passed:
+        read.wait()
+        write.start()
     for number, first, size, read, write in jobs:
         read.wait()
 
@@ -1315,8 +1320,8 @@
         write.start()
     for job in jobs:
         job[4].wait()
-    for copy in passed:
-        copy.wait()
+    for _, write in passed:
+        write.wait()
 
 
 def finish_outputs(sums, small, block_low, input_low, sizes):
@@ -1340,7 +1345,8 @@
         out_specs=tuple([anywhere] * count + [vmem] * 5 + [anywhere] * 2),
         scratch_shapes=[pltpu.VMEM(item.shape, low) for item in sums]
         + [pltpu.VMEM(item.shape, f32) for item in sums]
-        + [pltpu.SemaphoreType.DMA((jobs,)), pltpu.SemaphoreType.DMA((jobs,)), pltpu.SemaphoreType.DMA((2,))],
+        + [pltpu.VMEM(item.shape, item.dtype) for item in (block_low, input_low)]
+        + [pltpu.SemaphoreType.DMA((jobs,)), pltpu.SemaphoreType.DMA((jobs,)), pltpu.SemaphoreType.DMA((4,))],
         compiler_params=pltpu.CompilerParams(vmem_limit_bytes=56 * 1024 * 1024),
     )(*sums, small, block_low, input_low)
 

time: 448 us -> 337 us (0.75)
  Pallas kernels: 447 us -> 334 us
    pallas_call x1, Pallas kernels: 128 us -> 18.9 us  [finish_outputs(): pl.pallas_call(functools.partial(last_kernel, count), out_shape=tuple([sh...]
where the time goes in v4:
time: 337 us; the launch traced here: 335 us
  Pallas kernels  334 us (99%)
    pallas_call x1, Pallas kernels, backward(): pl.pallas_call(functools.partial(back_kernel, chunks, length), out_shape=...  286 us
    pallas_call x1, Pallas kernels, front(): pl.pallas_call(front_kernel, out_shape=tuple((item for item, _ in outs)),...  29.4 us
    pallas_call x1, Pallas kernels, finish_outputs(): pl.pallas_call(functools.partial(last_kernel, count), out_shape=tuple([sh...  18.9 us

profile of v4, /device:TPU:0, one launch (start us, length us, event | category | flops | bytes accessed | tf_op | source)
XLA Modules:
  0.0 335.3 jit_solution(5830645611756071823)
XLA Ops:
  0.6 29.4 %shard_map.254 = (bf16[768,896]{1,0:T(8,128)(2,1)}, f32[768,896]{1,0:T(8,128)}, bf16[896,768]{1,0:T(8,128)(2,1)}, bf16[6,64,1792]{2,1,0:T(8,128)(2,1)}, bf16[2,1...) custom-call(bf16[768,896]{1,0:T(8,128)(2,1)} %tokens_hbm.1, ...), custom_call_target="tpu_custom_call" | custom-call | tf_op jit(solution)/shard_map/pallas_call | solution.py:543
  30.0 286.3 %shard_map.255 = (bf16[768,896]{1,0:T(8,128)(2,1)}, f32[768,896]{1,0:T(8,128)}, bf16[448,4864]{1,0:T(8,128)(2,1)}, bf16[448,4864]{1,0:T(8,128)(2,1)}, bf16[2432,...) custom-call(bf16[768,896]{1,0:T(8,128)(2,1)} %get-tuple-element.56.h, ...), custom_call_target="tpu_custom_call" | custom-call | tf_op jit(solution)/shard_map/pallas_call | solution.py:1190
  316.3 18.9 %shard_map.256 = (f32[448,4864]{1,0:T(8,128)}, f32[448,4864]{1,0:T(8,128)}, f32[2432,896]{1,0:T(8,128)}, f32[448,896]{1,0:T(8,128)}, f32[448,896]{1,0:T(8,128)},...) custom-call(bf16[448,4864]{1,0:T(8,128)(2,1)} %get-tuple-element.74., ...), custom_call_target="tpu_custom_call" | custom-call | tf_op jit(solution)/shard_map/pallas_call | solution.py:1337

commit v5 on v4

--- a/solution.py
+++ b/solution.py
@@ -602,14 +602,7 @@
     angle_hbm,
     block_out,
     input_out,
-    gate_out,
-    up_out,
-    down_out,
-    query_out,
-    key_out,
-    value_out,
-    out_out,
-    small_out,
+    summed_out,
     acc,
     split,
     inward,
@@ -680,69 +673,11 @@
 
     small_chunk, small_lot, small_row = seat(2 * wide_blocks + 2)
 
-    def tile_writes(chunk):
-        found = []
-        for lot in (0, 1):
-            at = pl.multiple_of(chunk * LANES + lot * half_hidden, LANES)
-            for number, goal in enumerate((gate_out, up_out)):
-                found.append(
-                    pltpu.make_async_copy(
-                        acc.at[chunk, lot, pl.ds(number * share, share)],
-                        goal.at[:, pl.ds(at, LANES)],
-                        store.at[chunk, lot, number],
-                    )
-                )
-            for block in range(wide_blocks):
-                found.append(
-                    pltpu.make_async_copy(
-                        acc.at[chunk, lot, pl.ds(2 * share + block * tall, tall)],
-                        down_out.at[
-                            pl.ds(pl.multiple_of(chunk * LANES + lot * tall, tall), tall),
-                            pl.ds(block * LANES, LANES),
-                        ],
-                        store.at[chunk, lot, 2 + block],
-                    )
-                )
-        return found
-
-    def rest_writes(chunk):
-        goals = [(out_out, block) for block in range(wide_blocks)]
-        goals += [(key_out, 0), (value_out, 0)]
-        goals += [(query_out, block) for block in range(wide_blocks)]
-        found = []
-        for number, (goal, block) in enumerate(goals):
-            where, lot, row = seat(number)
-            if where == chunk:
-                found.append(
-                    pltpu.make_async_copy(
-                        acc.at[where, lot, pl.ds(row, share)],
-                        goal.at[:, pl.ds(block * LANES, LANES)],
-                        store.at[where, lot, row // share],
-                    )
-                )
-        if chunk == small_chunk:
-            for block in range(wide_blocks):
-                found.append(
-                    pltpu.make_async_copy(
-                        acc.at[chunk, small_lot, pl.ds(small_row + block * 16, 16)],
-                        small_out.at[:, pl.ds(block * LANES, LANES)],
-                        store.at[chunk, small_lot, 2 + block],
-                    )
-                )
-        return found
+    def write(chunk):
+        return pltpu.make_async_copy(acc.at[chunk], summed_out.at[chunk], store.at[chunk])
 
     def start_writes(chunk):
-        @pl.when(chunk < tiles)
-        def _():
-            for copy in tile_writes(chunk):
-                copy.start()
-
-        for rest in range(tiles, chunks):
-
-            @pl.when(chunk == rest)
-            def _():
-                for copy in rest_writes(rest):
-                    copy.start()
+        write(chunk).start()
 
     ladder = Ladder(chunks, length, acc, split, inward, mids, last, send, recv, freed, start_writes)
     enter(ladder, partner)
@@ -843,10 +778,10 @@
             gate_pre = dot(hidden, gate_buf[seat_of])
             up_pre = dot(hidden, up_buf[seat_of])
             grad = dot_nt(upstream[at], down_buf[seat_of])
-            sigmoid = 1.0 / (1.0 + jnp.exp(-gate_pre))
+            sigmoid = 0.5 + 0.5 * jnp.tanh(0.5 * gate_pre)
             swish = gate_pre * sigmoid
             unit = (swish * up_pre).astype(low)
-            gate_grad = (grad * up_pre * sigmoid * (1.0 + gate_pre * (1.0 - sigmoid))).astype(low)
+            gate_grad = (grad * up_pre * (sigmoid + swish * (1.0 - sigmoid))).astype(low)
             up_grad = (grad * swish).astype(low)
             product[at] = unit
             gate_back[at] = gate_grad
@@ -861,7 +796,7 @@
             some = product_turned[span(owner, LANES)]
             put_down(target, where, dot(some, upstream[...]))
 
-    paced = 12
+    pace = 2
 
     def tile_step(tile, carry):
         for copy in loads(tile):
@@ -880,18 +815,18 @@
 
         across(tile).start()
 
-        before, after = lax.div(tile * paced, tiles), lax.div((tile + 1) * paced, tiles)
-
-        @pl.when(after > before)
+        @pl.when(lax.rem(tile, pace) == pace - 1)
         def _():
-            tick(before)
+            tick(lax.div(tile, pace))
 
         return carry
 
     lax.fori_loop(0, tiles, tile_step, 0)
-    clock = paced
+    clock = tiles // pace
 
     finish(tiles - 1)
+    tick(clock)
+    clock += 1
     for copy in early:
         copy.wait()
     gain_sum[...] = jnp.zeros_like(gain_sum)
@@ -948,6 +883,8 @@
     next_mat.start()
     next_turned = pltpu.make_async_copy(turned_hbm, hidden_turned, plain.at[2])
     next_turned.start()
+    tick(clock)
+    clock += 1
     block_write.wait()
     tokens_load = pltpu.make_async_copy(tokens_hbm, tokens, plain.at[0])
     tokens_load.start()
@@ -979,7 +916,7 @@
         pair_sum[0, rows_of, at] += dot_nt(queries[index], score_grad[...])
         query_sum[...] += dot(keys_turned[rows_of, at], score_grad[...])
 
-    beat = 5
+    beat = 4
 
     def attend_step(step, carry):
         group, inside = lax.div(step, per_group), lax.rem(step, per_group)
@@ -1118,14 +1055,10 @@
         pair_push.wait_send()
 
     def drain(chunk, carry):
-        for copy in tile_writes(chunk):
-            copy.wait()
+        write(chunk).wait()
         return carry
 
-    lax.fori_loop(0, tiles, drain, 0)
-    for chunk in range(tiles, chunks):
-        for copy in rest_writes(chunk):
-            copy.wait()
+    lax.fori_loop(0, chunks, drain, 0)
 
 
 def backward(front_parts, upstream, tokens, angles, gate_w, up_w, down_w, replicas, spread):
@@ -1192,17 +1125,10 @@
         out_shape=(
             shape((rows, width), low),
             shape((rows, width), f32),
-            shape((width // 2, columns), low),
-            shape((width // 2, columns), low),
-            shape((columns // 2, width), low),
-            shape((width // 2, H * HD), low),
-            shape((width // 2, kv_width), low),
-            shape((width // 2, kv_width), low),
-            shape((H * HD // 2, width), low),
-            shape((16, width), low),
+            shape((chunks, 2, ROWS, LANES), low),
         ),
         in_specs=[vmem] * 3 + [anywhere] * (len(inputs) - 3),
-        out_specs=(anywhere,) * 10,
+        out_specs=(anywhere,) * 3,
         scratch_shapes=[
             pltpu.VMEM((chunks, 2, ROWS, LANES), low),
             pltpu.VMEM((4, 2, HALF, LANES), low),
@@ -1250,7 +1176,7 @@
             pltpu.SemaphoreType.DMA((2,)),
             pltpu.SemaphoreType.DMA((2,)),
             pltpu.SemaphoreType.DMA((AHEAD + 1, 10)),
-            pltpu.SemaphoreType.DMA((chunks, 2, 2 + width // LANES)),
+            pltpu.SemaphoreType.DMA((chunks,)),
             pltpu.SemaphoreType.DMA((12,)),
             pltpu.SemaphoreType.DMA,
             pltpu.SemaphoreType.DMA,
@@ -1261,94 +1187,173 @@
     )(*inputs)
 
 
-SLAB = 64
-
-
-def last_kernel(count, *refs):
-    sources, small, block_low, input_low = refs[:count], refs[count], refs[count + 1], refs[count + 2]
-    outs = refs[count + 3 :]
-    goals, lines, block_out, input_out = outs[:count], outs[count : count + 5], outs[count + 5], outs[count + 6]
-    rest = outs[count + 7 :]
-    narrow, wide = rest[:count], rest[count : 2 * count]
-    block_held, input_held, load, store, plain = rest[2 * count :]
+def last_kernel(
+    summed,
+    block_low,
+    input_low,
+    gate_out,
+    up_out,
+    down_out,
+    query_out,
+    out_out,
+    key_out,
+    value_out,
+    first_gain_out,
+    query_bias_out,
+    key_bias_out,
+    value_bias_out,
+    second_gain_out,
+    block_out,
+    input_out,
+    narrow,
+    gate,
+    up,
+    down,
+    query,
+    out,
+    key,
+    value,
+    block_held,
+    input_held,
+    load,
+    store,
+    plain,
+):
     rank = lax.axis_index("group")
+    f32 = jnp.float32
+    chunks = summed.shape[0]
+    share, columns = gate_out.shape
+    width = down_out.shape[1]
+    wide_blocks = width // LANES
+    half_hidden = columns // 2
+    tiles = half_hidden // LANES
+    tall = LANES // 2
     passed = [
-        (pltpu.make_async_copy(source, held, plain.at[2 * number]), pltpu.make_async_copy(held, goal, plain.at[2 * number + 1]))
+        (
+            pltpu.make_async_copy(source, held, plain.at[2 * number]),
+            pltpu.make_async_copy(held, goal, plain.at[2 * number + 1]),
+        )
         for number, (source, held, goal) in enumerate(
             ((block_low, block_held, block_out), (input_low, input_held, input_out))
         )
     ]
-    jobs = []
-    for number, source in enumerate(sources):
-        rows, columns = source.shape
-        size = SLAB * max(1, 4864 // columns)
-        for first in range(0, rows, size):
-            at = pl.ds(first, min(size, rows - first))
-            place = len(jobs)
-            jobs.append(
-                (
-                    number,
-                    first,
-                    min(size, rows - first),
-                    pltpu.make_async_copy(source.at[at], narrow[number].at[at], load.at[place]),
-                    pltpu.make_async_copy(wide[number].at[at], goals[number].at[at], store.at[place]),
-                )
-            )
-    for read, _ in passed:
-        read.start()
-    for job in jobs:
-        job[3].start()
-    for line, (row, first, goal) in enumerate(
-        ((0, 0, lines[0]), (1, 0, lines[1]), (2, 0, lines[2]), (2, KVH * HD, lines[3]), (3, 0, lines[4]))
+    rest = [
+        pltpu.make_async_copy(source, goal, plain.at[4 + number])
+        for number, (source, goal) in enumerate(((query, query_out), (out, out_out), (key, key_out), (value, value_out)))
+    ]
+
+    def seat(number):
+        lot, place = divmod(number, 3)
+        return tiles + lot // 2, lot % 2, place * share
+
+    def rest_block(number):
+        chunk, lot, row = seat(number)
+        return narrow[chunk, lot, pl.ds(row, share)].astype(f32)
+
+    def read(chunk):
+        return pltpu.make_async_copy(summed.at[chunk], narrow.at[chunk], load.at[chunk])
+
+    def writes(tile):
+        found = []
+        for lot in (0, 1):
+            at = pl.ds(pl.multiple_of(tile * LANES + lot * half_hidden, LANES), LANES)
+            for held, goal in ((gate, gate_out), (up, up_out)):
+                found.append(pltpu.make_async_copy(held.at[:, at], goal.at[:, at], store.at[tile, len(found)]))
+        at = span(tile, LANES)
+        found.append(pltpu.make_async_copy(down.at[at], down_out.at[at], store.at[tile, 4]))
+        return found
+
+    for first, _ in passed:
+        first.start()
+    for chunk in range(chunks):
+        read(chunk).start()
+    for first, second in passed:
+        first.wait()
+        second.start()
+
+    def place(tile, carry):
+        read(tile).wait()
+        for lot in (0, 1):
+            at = pl.ds(pl.multiple_of(tile * LANES + lot * half_hidden, LANES), LANES)
+            for number, held in enumerate((gate, up)):
+                some = pl.ds(number * share, share)
+                held[:, at] = narrow[tile, lot, some].astype(f32)
+            goal_rows = pl.ds(pl.multiple_of(tile * LANES + lot * tall, tall), tall)
+            for block in range(wide_blocks):
+                some = pl.ds(2 * share + block * tall, tall)
+                down[goal_rows, block * LANES : (block + 1) * LANES] = narrow[tile, lot, some].astype(f32)
+        for copy in writes(tile):
+            copy.start()
+        return carry
+
+    lax.fori_loop(0, tiles, place, 0)
+    for chunk in range(tiles, chunks):
+        read(chunk).wait()
+    for block in range(wide_blocks):
+        at = slice(block * LANES, (block + 1) * LANES)
+        out[:, at] = rest_block(block)
+        query[:, at] = rest_block(wide_blocks + 2 + block)
+    key[...] = rest_block(wide_blocks)
+    value[...] = rest_block(wide_blocks + 1)
+    for copy in rest:
+        copy.start()
+    small_chunk, small_lot, small_row = seat(2 * wide_blocks + 2)
+    small = jnp.concatenate(
+        [narrow[small_chunk, small_lot, pl.ds(small_row + 16 * block, 16)] for block in range(wide_blocks)], axis=1
+    ).astype(f32)
+    for row, first, goal in (
+        (0, 0, first_gain_out),
+        (1, 0, query_bias_out),
+        (2, 0, key_bias_out),
+        (2, KVH * HD, value_bias_out),
+        (3, 0, second_gain_out),
     ):
         size = goal.shape[0]
-        both = small[...][row : row + 1].astype(jnp.float32)
-        mine = jnp.where(rank == 0, both[:, first : first + size], both[:, first + size : first + 2 * size])
+        line = small[row : row + 1]
+        mine = jnp.where(rank == 0, line[:, first : first + size], line[:, first + size : first + 2 * size])
         goal[...] = mine.reshape(size)
-    for read, write in passed:
-        read.wait()
-        write.start()
-    for number, first, size, read, write in jobs:
-        read.wait()
-
-        def cast(step, carry):
-            at = pl.ds(pl.multiple_of(first + step * 32, 32), 32)
-            wide[number][at] = narrow[number][at].astype(jnp.float32)
-            return carry
-
-        lax.fori_loop(0, size // 32, cast, 0)
-        write.start()
-    for job in jobs:
-        job[4].wait()
-    for _, write in passed:
-        write.wait()
-
-
-def finish_outputs(sums, small, block_low, input_low, sizes):
+
+    def drain(tile, carry):
+        for copy in writes(tile):
+            copy.wait()
+        return carry
+
+    lax.fori_loop(0, tiles, drain, 0)
+    for copy in rest:
+        copy.wait()
+    for _, second in passed:
+        second.wait()
+
+
+def finish_outputs(summed, block_low, input_low, columns, sizes):
     low, f32 = jnp.bfloat16, jnp.float32
+    width = block_low.shape[1]
+    share, heads, kv_width = width // 2, H * HD, KVH * HD
+    tiles = columns // (2 * LANES)
     anywhere = pl.BlockSpec(memory_space=pl.ANY)
     vmem = pl.BlockSpec(memory_space=pltpu.VMEM)
     shape = jax.ShapeDtypeStruct
-    count = len(sums)
-    jobs = 0
-    for item in sums:
-        rows, columns = item.shape
-        jobs += -(-rows // (SLAB * max(1, 4864 // columns)))
+    mats = ((share, columns), (share, columns), (columns // 2, width), (share, heads), (heads // 2, width))
+    mats += ((share, kv_width), (share, kv_width))
     return pl.pallas_call(
-        functools.partial(last_kernel, count),
+        last_kernel,
         out_shape=tuple(
-            [shape(item.shape, f32) for item in sums]
+            [shape(item, f32) for item in mats]
             + [shape((size,), f32) for size in sizes]
             + [shape(block_low.shape, block_low.dtype), shape(input_low.shape, input_low.dtype)]
         ),
-        in_specs=[anywhere] * count + [vmem] + [anywhere] * 2,
-        out_specs=tuple([anywhere] * count + [vmem] * 5 + [anywhere] * 2),
-        scratch_shapes=[pltpu.VMEM(item.shape, low) for item in sums]
-        + [pltpu.VMEM(item.shape, f32) for item in sums]
+        in_specs=[anywhere] * 3,
+        out_specs=tuple([anywhere] * 7 + [vmem] * 5 + [anywhere] * 2),
+        scratch_shapes=[pltpu.VMEM(summed.shape, low)]
+        + [pltpu.VMEM(item, f32) for item in mats]
         + [pltpu.VMEM(item.shape, item.dtype) for item in (block_low, input_low)]
-        + [pltpu.SemaphoreType.DMA((jobs,)), pltpu.SemaphoreType.DMA((jobs,)), pltpu.SemaphoreType.DMA((4,))],
-        compiler_params=pltpu.CompilerParams(vmem_limit_bytes=56 * 1024 * 1024),
-    )(*sums, small, block_low, input_low)
+        + [
+            pltpu.SemaphoreType.DMA((summed.shape[0],)),
+            pltpu.SemaphoreType.DMA((tiles, 5)),
+            pltpu.SemaphoreType.DMA((8,)),
+        ],
+        compiler_params=pltpu.CompilerParams(vmem_limit_bytes=60 * 1024 * 1024),
+    )(summed, block_low, input_low)
 
 
 def local(
@@ -1387,14 +1392,7 @@
     (
         block_output,
         input_grad,
-        gate_sum,
-        up_sum,
-        down_sum,
-        query_sum,
-        key_sum,
-        value_sum,
-        out_sum,
-        small,
+        summed,
     ) = backward(
         parts, cotangent, tokens, angles, gate_weight, up_weight, down_weight, lax.axis_size("replica"), spread
     )
@@ -1415,9 +1413,7 @@
         second_gain_grad,
         block_output,
         input_grad,
-    ) = finish_outputs(
-        (gate_sum, up_sum, down_sum, query_sum, out_sum, key_sum, value_sum), small, block_output, input_grad, sizes
-    )
+    ) = finish_outputs(summed, block_output, input_grad, gate_weight.shape[1], sizes)
     return (
         block_output,
         input_grad,

time: 337 us -> 332 us (0.985)
    pallas_call x1, Pallas kernels: 286 us -> 283 us  [backward(): pl.pallas_call(functools.partial(back_kernel, chunks, length), out_shape=...]
where the time goes in v5:
time: 332 us
  Pallas kernels  331 us (100%)
    pallas_call x1, Pallas kernels, backward(): pl.pallas_call(functools.partial(back_kernel, chunks, length), out_shape=...  283 us
    pallas_call x1, Pallas kernels, front(): pl.pallas_call(front_kernel, out_shape=tuple((item for item, _ in outs)),...  29.4 us
    pallas_call x1, Pallas kernels, finish_outputs(): pl.pallas_call(last_kernel, out_shape=tuple([shape(item, f32) for item in...  18.6 us

profile of v5, /device:TPU:0, one launch (start us, length us, event | category | flops | bytes accessed | tf_op | source)
XLA Modules:
  0.0 331.7 jit_solution(15456781331317904598)
XLA Ops:
  0.6 29.4 %shard_map.254 = (bf16[768,896]{1,0:T(8,128)(2,1)}, f32[768,896]{1,0:T(8,128)}, bf16[896,768]{1,0:T(8,128)(2,1)}, bf16[6,64,1792]{2,1,0:T(8,128)(2,1)}, bf16[2,1...) custom-call(bf16[768,896]{1,0:T(8,128)(2,1)} %tokens_hbm.1, ...), custom_call_target="tpu_custom_call" | custom-call | tf_op jit(solution)/shard_map/pallas_call | solution.py:543
  30.1 282.9 %shard_map.255 = (bf16[768,896]{1,0:T(8,128)(2,1)}, f32[768,896]{1,0:T(8,128)}, bf16[22,2,1344,128]{3,2,1,0:T(8,128)(2,1)}) custom-call(bf16[768,896]{1,0:T(8,128)(2,1)} %get-tuple-element.49.hidden_two, bf16[768,896]{1,0:T(8,128)(2,1)} %upstream.1, f32[8,896]{1,0:T(8,128)} %get-tuple-element.50.vectors, bf16[768,896]{1,0:T(8,128)(2,1)} %tokens_hbm.1, ...), custom_call_target="tpu_custom_call" | custom-call | tf_op jit(solution)/shard_map/pallas_call | solution.py:1123
  313.0 18.6 %shard_map.256 = (f32[448,4864]{1,0:T(8,128)}, f32[448,4864]{1,0:T(8,128)}, f32[2432,896]{1,0:T(8,128)}, f32[448,896]{1,0:T(8,128)}, f32[448,896]{1,0:T(8,128)},...) custom-call(bf16[22,2,1344,128]{3,2,1,0:T(8,128)(2,1)} %get-tuple-el, ...), custom_call_target="tpu_custom_call" | custom-call | tf_op jit(solution)/shard_map/pallas_call | solution.py:1338

commit v6 on v5

--- a/solution.py
+++ b/solution.py
@@ -680,7 +680,6 @@
         write(chunk).start()
 
     ladder = Ladder(chunks, length, acc, split, inward, mids, last, send, recv, freed, start_writes)
-    enter(ladder, partner)
     tick = ladder.tick
 
     early = [
@@ -757,6 +756,7 @@
     for block in range(blocks):
         at = slice(block * BLOCK, (block + 1) * BLOCK)
         turned[:, at] = hidden_two[at].T
+    enter(ladder, partner)
 
     def put(target, where, value, first_row):
         for lot in (0, 1):
@@ -911,10 +911,10 @@
         weights_grad = dot(values[group, at], heads_grad[index])
         probs[...] = weights.astype(low)
         score_grad[...] = (weights * (weights_grad - delta[index])).astype(low)
-        rows_of = span(group, HD)
-        pair_sum[1, rows_of, at] += dot_nt(heads_grad[index], probs[...])
-        pair_sum[0, rows_of, at] += dot_nt(queries[index], score_grad[...])
-        query_sum[...] += dot(keys_turned[rows_of, at], score_grad[...])
+        pair_sum[group, at] += jnp.concatenate(
+            [dot_nt(score_grad[...], queries[index]), dot_nt(probs[...], heads_grad[index])], axis=1
+        )
+        query_sum[...] += dot(keys_turned[span(group, HD), at], score_grad[...])
 
     beat = 4
 
@@ -960,7 +960,7 @@
     clock += steps // beat
 
     pair_push = pltpu.make_async_remote_copy(
-        src_ref=pair_sum.at[:, :, pl.ds(0, rows)],
+        src_ref=pair_sum.at[:, pl.ds(0, rows)],
         dst_ref=pair_far,
         send_sem=psend,
         recv_sem=precv,
@@ -986,13 +986,14 @@
     @pl.when(rank == 0)
     def _():
         pair_push.wait_recv()
-        pair_sum[:, :, :rows] += pair_far[...]
+        pair_sum[:, :rows] += pair_far[...]
 
     own = span(rank, rows)
     for head in range(KVH):
         at = slice(head * HD, (head + 1) * HD)
-        pair_low[0, at] = turn_back(pair_sum[0, at, own], angles[0], angles[1]).astype(low)
-    pair_low[1] = pair_sum[1, :, own].astype(low)
+        both = pair_sum[head, own].T
+        pair_low[0, at] = turn_back(both[:HD], angles[0], angles[1]).astype(low)
+        pair_low[1, at] = both[HD:].astype(low)
     for owner, target, mine in both_sides:
         some = hidden_turned[pl.ds(pl.multiple_of(owner * share, 16), share)]
         scatter(wide_blocks, dot_nt(some, pair_low[0]), target, mine)
@@ -1166,8 +1167,8 @@
             pltpu.VMEM((BLOCK, queries.shape[2]), low),
             pltpu.VMEM((BLOCK, queries.shape[2]), low),
             pltpu.VMEM(queries.shape[1:], f32),
-            pltpu.VMEM((2, kv_width, rows * spread), f32),
-            pltpu.VMEM((2, kv_width, rows), f32),
+            pltpu.VMEM((KVH, rows * spread, 2 * HD), f32),
+            pltpu.VMEM((KVH, rows, 2 * HD), f32),
             pltpu.VMEM((2, kv_width, rows), low),
             pltpu.VMEM((8, width), f32),
             pltpu.SemaphoreType.DMA((7, slots, 2)),

time: 332 us -> 331 us (level)
  no operation moved by 1% of the time
where the time goes in v6:
time: 331 us
  Pallas kernels  330 us (100%)
    pallas_call x1, Pallas kernels, backward(): pl.pallas_call(functools.partial(back_kernel, chunks, length), out_shape=...  282 us
    pallas_call x1, Pallas kernels, front(): pl.pallas_call(front_kernel, out_shape=tuple((item for item, _ in outs)),...  29.4 us
    pallas_call x1, Pallas kernels, finish_outputs(): pl.pallas_call(last_kernel, out_shape=tuple([shape(item, f32) for item in...  18.6 us

profile of v6, /device:TPU:0, one launch (start us, length us, event | category | flops | bytes accessed | tf_op | source)
XLA Modules:
  0.0 331.0 jit_solution(4110072017913583309)
XLA Ops:
  0.6 29.4 %shard_map.254 = (bf16[768,896]{1,0:T(8,128)(2,1)}, f32[768,896]{1,0:T(8,128)}, bf16[896,768]{1,0:T(8,128)(2,1)}, bf16[6,64,1792]{2,1,0:T(8,128)(2,1)}, bf16[2,1...) custom-call(bf16[768,896]{1,0:T(8,128)(2,1)} %tokens_hbm.1, ...), custom_call_target="tpu_custom_call" | custom-call | tf_op jit(solution)/shard_map/pallas_call | solution.py:543
  30.1 282.2 %shard_map.255 = (bf16[768,896]{1,0:T(8,128)(2,1)}, f32[768,896]{1,0:T(8,128)}, bf16[22,2,1344,128]{3,2,1,0:T(8,128)(2,1)}) custom-call(bf16[768,896]{1,0:T(8,128)(2,1)} %get-tuple-element.49.hidden_two, bf16[768,896]{1,0:T(8,128)(2,1)} %upstream.1, f32[8,896]{1,0:T(8,128)} %get-tuple-element.50.vectors, bf16[768,896]{1,0:T(8,128)(2,1)} %tokens_hbm.1, ...), custom_call_target="tpu_custom_call" | custom-call | tf_op jit(solution)/shard_map/pallas_call | solution.py:1124
  312.3 18.6 %shard_map.256 = (f32[448,4864]{1,0:T(8,128)}, f32[448,4864]{1,0:T(8,128)}, f32[2432,896]{1,0:T(8,128)}, f32[448,896]{1,0:T(8,128)}, f32[448,896]{1,0:T(8,128)},...) custom-call(bf16[22,2,1344,128]{3,2,1,0:T(8,128)(2,1)} %get-tuple-el, ...), custom_call_target="tpu_custom_call" | custom-call | tf_op jit(solution)/shard_map/pallas_call | solution.py:1339
